TPU v7x, 512 devices: a whole 4x4x16 slice. The times are simulated.
512 devices in a mesh: seq: 32 (over x, z_hi, core), col: 16 (over y, z_lo).
Axes of the slice: x: 4, y: 4, z: 16 (z_hi: 4, z_lo: 4; z = z_hi * 4 + z_lo), core: 2. Of those that a mesh axis runs over, the one named last changes fastest.
Arguments:
- alignment_embedding_tensor: bfloat16 [512, 128, 768], P('seq', 'col'), may hold values from -3 to 3
- horizontal_attention_triples: bfloat16 [512, 128, 2304], P('seq', 'col'), may hold values from -10 to 10
- occupancy_indicator: int32 [512, 128], P('seq', 'col'), may hold values from 0 to 1, as said below
- horizontal_attention_exit_matrix: bfloat16 [768, 768], P('col'), may hold values from -0.21875 to 0.21875
- vertical_attention_entry_matrix: bfloat16 [768, 2304], P('col'), may hold values from -0.43164062 to 0.43164062
- vertical_attention_exit_matrix: bfloat16 [768, 768], P('col'), may hold values from -0.21875 to 0.21875
- vertical_layernorm_scaling: float32 [768], replicated, may hold values from 0.25 to 1.75
Outputs:
- mixed: float32 [512, 128, 768], P('seq', 'col')
Inputs may be any that keep to these rules, and one draw needn't show every extreme that they name: `occupancy_indicator`: every column holds a residue in some sequence.
All inputs are finite; a program needn't handle non-finite values.
Results may differ from a plain program's by a relative error of at most 0.035.
Values may be sent and summed in bfloat16 or wider, within the bound.
A program may use at most 64 MiB of HBM per device.

v0:
```python
import math

import jax
import jax.numpy as jnp
from jax import lax
from jax.sharding import Mesh
from jax.sharding import PartitionSpec as P

H = 12
DH = 64
COL = ("col_0", "col_1")


def in_one_piece(arrays, axis, dim, along):
    ends, at = ([], 0)
    for a in arrays[:-1]:
        at += a.shape[along]
        ends.append(at)
    both = jnp.concatenate(arrays, axis=along)
    return tuple(jnp.split(lax.all_gather(both, axis, axis=dim, tiled=True), ends, axis=along))


def from_everyone(array, axis):
    length = lax.axis_size(axis)
    return lax.all_to_all(
        jnp.broadcast_to(array[None], (length, *array.shape)), axis, 0, 0, tiled=True
    )


def of_everyone(array, axis):
    return from_everyone(array, axis).sum(axis=0)


def whole_of(array, axes, dim):
    filled = array
    for number in range(len(axes) - 1, -1, -1):
        filled = lax.all_gather(filled, axes[number], axis=dim, tiled=True)
    return filled


def items_in_groups(array, axis, split_dim, concat_dim, work, item_dim, out_dim):
    items = jax.tree.leaves(array)[0].shape[item_dim]
    count = 2 if items % 2 == 0 else 1
    gathered = []
    for k in range(count):
        group = jax.tree.map(
            lambda a: lax.slice_in_dim(
                a, k * (items // count), (k + 1) * (items // count), axis=item_dim
            ),
            array,
        )
        gathered.append(
            work(
                lax.all_to_all(
                    group, axis, split_axis=split_dim, concat_axis=concat_dim, tiled=True
                )
            )
        )
    return jax.tree.map(lambda *parts: jnp.concatenate(parts, axis=out_dim), *gathered)


def attend_columns(pieces):
    block, keep = pieces
    cq = block[..., :DH]
    ck = block[..., DH : 2 * DH]
    cv = block[..., 2 * DH :]
    scores = jnp.einsum("rgud,sgud->gurs", cq, ck, preferred_element_type=jnp.float32) / math.sqrt(
        DH
    )
    mask_keys = jnp.transpose(keep, (1, 2, 0))[:, :, None, :]
    scores = jnp.where(mask_keys > 0, scores, -1000000000.0)
    probs = jax.nn.softmax(scores, axis=-1).astype(jnp.bfloat16)
    return jnp.einsum("gurs,sgud->rgud", probs, cv, preferred_element_type=jnp.float32).astype(
        jnp.bfloat16
    )


def per_device(
    alignment_embedding_tensor,
    horizontal_attention_triples,
    occupancy_indicator,
    horizontal_attention_exit_matrix,
    vertical_attention_entry_matrix,
    vertical_attention_exit_matrix,
    vertical_layernorm_scaling,
):
    protein_extent, site_extent, embedding_dimension = alignment_embedding_tensor.shape
    total_rows = protein_extent * lax.axis_size("seq")
    live = occupancy_indicator.astype(jnp.bfloat16)
    parts = horizontal_attention_triples.reshape(protein_extent, site_extent, 3, H, DH)
    query = parts[:, :, 0] * live[:, :, None, None]
    keys = parts[:, :, 1]
    values = parts[:, :, 2]
    scale = 1.0 / (math.sqrt(DH) * math.sqrt(total_rows))
    full_wo_row, full_qkv, full_wo_col = in_one_piece(
        (
            horizontal_attention_exit_matrix,
            vertical_attention_entry_matrix,
            vertical_attention_exit_matrix,
        ),
        COL,
        0,
        1,
    )
    all_keys = lax.all_gather(keys, COL, axis=1, tiled=True)
    partial_value = (
        jnp.einsum("rihd,rjhd->hij", query, all_keys, preferred_element_type=jnp.float32) * scale
    )
    logits = of_everyone(partial_value, "seq")
    all_values = whole_of(values, COL, 1)
    row_probs = jax.nn.softmax(logits, axis=-1).astype(jnp.bfloat16)
    context = jnp.einsum(
        "hij,rjhd->rihd", row_probs, all_values, preferred_element_type=jnp.float32
    ).astype(jnp.bfloat16)
    merged_attended_heads = context.reshape(protein_extent * site_extent, embedding_dimension)
    skip_connection_hidden = alignment_embedding_tensor.reshape(
        protein_extent * site_extent, embedding_dimension
    ).astype(jnp.float32) + jnp.dot(
        merged_attended_heads, full_wo_row, preferred_element_type=jnp.float32
    )
    center = skip_connection_hidden - jnp.mean(skip_connection_hidden, axis=-1, keepdims=True)
    variance = jnp.mean(center * center, axis=-1, keepdims=True)
    normed = (center * lax.rsqrt(variance + 1e-05) * vertical_layernorm_scaling).astype(
        jnp.bfloat16
    )
    col_qkv = jnp.dot(normed, full_qkv, preferred_element_type=jnp.float32).astype(jnp.bfloat16)
    seq_count = lax.axis_size("seq")
    units = site_extent * H // seq_count
    col_qkv = jnp.transpose(col_qkv.reshape(protein_extent, site_extent, 3, H, DH), (0, 1, 3, 2, 4))
    col_qkv = col_qkv.reshape(protein_extent, seq_count, units, 3 * DH)
    live_units = jnp.broadcast_to(live[:, :, None], (protein_extent, site_extent, H)).reshape(
        protein_extent, seq_count, units
    )
    attended = items_in_groups((col_qkv, live_units), "seq", 1, 0, attend_columns, 2, 2)
    returned_cols = lax.all_to_all(attended, "seq", split_axis=0, concat_axis=1, tiled=True)
    col_context = returned_cols.reshape(protein_extent * site_extent, embedding_dimension)
    mixed = skip_connection_hidden + jnp.dot(
        col_context, full_wo_col, preferred_element_type=jnp.float32
    )
    return mixed.reshape(protein_extent, site_extent, embedding_dimension)


def solution(mesh):
    torus = Mesh(mesh.devices.reshape(mesh.shape["seq"], 4, 4), ("seq", "col_0", "col_1"))
    in_specs = (
        P("seq", COL, None),
        P("seq", COL, None),
        P("seq", COL),
        P(COL, None),
        P(COL, None),
        P(COL, None),
        P(),
    )
    out_specs = P("seq", COL, None)
    return jax.shard_map(
        per_device, mesh=torus, in_specs=in_specs, out_specs=out_specs, check_vma=False
    )
```

profile of v0, /device:TPU:1, one launch (start us, length us, event | category | flops | bytes accessed | tf_op | source)
XLA Modules:
  0.0 497.0 jit_solution(10762542921084627330)
XLA Ops:
  6.5 1.9 reshape.85
  8.5 0.3 fusion.40
  8.8 1.0 copy.42
  9.9 0.3 copy.45
  10.2 37.4 %all-gather.1 = bf16[16,32,1,12,64]{4,0,3,2,1:T(8,128)(2,1)} all-gather(bf16[16,8,1,12,64]{4,0,3,2,1:T(8,128)(2,1)S(1)} %copy.45), channel_id=3, replica_groups=mesh['seq'=32,'col_0'=4,'col_1'=4] {'col_1'}, dimensions={1}, use_global_device_ids=true | all-gather | bytes 983040 | tf_op jit(solution)/shard_map/all_gather | solution.py:37
  47.5 0.0 all-gather.7.cloned.1.call-start
  47.6 0.8 pad_maximum_fusion
  48.5 0.1 copy.41
  48.5 1.0 fusion.31
  49.6 124.1 %all-gather.9.cloned.1.call-done = bf16[16,128,1,12,64]{4,0,3,2,1:T(8,128)(2,1)} async-done(((bf16[16,8,1,12,64]{4,0,3,2,1:T(8,128)(2,1)}), bf16[16,128,1,12,64]{4,0,3,2,1:T(8,128)(2,1)}) %all-gather.9.cloned.1.call-update) | async-done | bytes 3145744 | tf_op jit(solution)/shard_map/all_gather | solution.py:105
  173.6 7.9 %copy.43 = bf16[16,128,1,12,64]{1,4,0,3,2:T(8,128)(2,1)S(1)} copy(bf16[16,128,1,12,64]{4,0,3,2,1:T(8,128)(2,1)} %all-gather.9.cloned.1.call-done) | data formatting | bytes 6291456 | tf_op jit(solution)/shard_map/all_gather | solution.py:105
  181.6 1.6 fusion.28
  183.2 1.4 broadcast_in_dim.16
  184.6 17.1 %all-to-all-start = ((f32[32,12,8,128]{3,2,1,0:T(8,128)}), f32[32,12,8,128]{3,2,1,0:T(8,128)}, u32[]{:S(2)}, u32[]{:S(2)}) async-start(f32[32,12,8,128]{3,2,1,0:T(8,128)} %broadcast_in_dim.16), calls=%async_computation | async-start | bytes 3145728 | tf_op jit(solution)/shard_map/all_to_all | solution.py:25
  201.8 48.3 %all-gather.11.cloned.1.call-done = bf16[16,128,1,12,64]{4,0,3,2,1:T(8,128)(2,1)} async-done(((bf16[16,32,1,12,64]{4,0,3,2,1:T(8,128)(2,1)}), bf16[16,128,1,12,64]{4,0,3,2,1:T(8,128)(2,1)}) %all-gather.11.cloned.1.call-update) | async-done | bytes 3145744 | tf_op jit(solution)/shard_map/all_gather | solution.py:37
  250.1 7.9 %copy.46 = bf16[16,128,1,12,64]{1,4,0,3,2:T(8,128)(2,1)S(1)} copy(bf16[16,128,1,12,64]{4,0,3,2,1:T(8,128)(2,1)} %all-gather.11.cloned.1.call-done) | data formatting | bytes 6291456 | tf_op jit(solution)/shard_map/all_gather | solution.py:37
  258.0 19.1 %all-to-all-done = f32[32,12,8,128]{3,2,1,0:T(8,128)} async-done(((f32[32,12,8,128]{3,2,1,0:T(8,128)}), f32[32,12,8,128]{3,2,1,0:T(8,128)}, u32[]{:S(2)}, u32[]{:S(2)}) %all-to-all-start) | async-done | bytes 1572896 | tf_op jit(solution)/shard_map/all_to_all | solution.py:25
  277.2 0.6 broadcast_in_dim.23
  277.8 7.0 %all-to-all-start.2 = ((bf16[16,32,3]{0,2,1:T(4,128)(2,1)}), bf16[16,32,3]{0,2,1:T(4,128)(2,1)}, u32[]{:S(2)}, u32[]{:S(2)}) async-start(bf16[16,32,3]{0,2,1:T(4,128)(2,1)} %broadcast_in_dim.23), calls=%async_computation.2 | async-start | bytes 65536 | tf_op jit(solution)/shard_map/all_to_all | solution.py:54
  284.9 1.5 reduce_sum.45
  286.4 0.6 copy-done
  287.0 0.2 fusion.41
  287.2 3.4 fusion.16
  290.6 0.3 copy.47
  290.9 0.3 reshape.86
  291.2 104.0 %all-gather.7.cloned.1.call-done = bf16[768,3840]{1,0:T(8,128)(2,1)} async-done(((bf16[48,3840]{1,0:T(8,128)(2,1)}), bf16[768,3840]{1,0:T(8,128)(2,1)}) %all-gather.7.cloned.1.call-update) | async-done | bytes 5898256 | tf_op jit(solution)/shard_map/all_gather | solution.py:20
  395.2 1.7 fusion.42
  396.9 0.2 multiply_reduce_fusion
  397.1 2.7 convolution_convert_fusion
  399.8 1.0 reshape.87
  400.8 0.8 copy.48
  401.7 2.0 reshape.88
  403.7 13.0 %all-to-all-start.1 = ((bf16[16,32,3,192]{3,0,2,1:T(8,128)(2,1)}), bf16[16,32,3,192]{3,0,2,1:T(8,128)(2,1)S(1)}, u32[]{:S(2)}, u32[]{:S(2)}) async-start(bf16[16,32,3,192]{3,0,2,1:T(8,128)(2,1)} %reshape.88), calls=%async_computation.1 | async-start | bytes 1572864 | tf_op jit(solution)/shard_map/all_to_all | solution.py:54
  416.7 0.8 compare_bitcast_fusion
  417.5 0.1 gt.26
  417.6 41.3 %all-to-all-done.1 = bf16[16,32,3,192]{3,0,2,1:T(8,128)(2,1)S(1)} async-done(((bf16[16,32,3,192]{3,0,2,1:T(8,128)(2,1)}), bf16[16,32,3,192]{3,0,2,1:T(8,128)(2,1)S(1)}, u32[]{:S(2)}, u32[]{:S(2)}) %all-to-all-start.1) | async-done | bytes 589856 | tf_op jit(solution)/shard_map/all_to_all | solution.py:54
  458.9 0.1 copy.49
  459.0 0.6 fusion.32
  459.6 1.3 fusion.43
  460.9 0.5 fusion.22
  461.3 0.3 copy.55
  461.7 0.4 reshape.102
  462.0 25.0 %all_to_all.50 = bf16[32,2,1536]{2,1,0:T(2,128)(2,1)S(1)} all-to-all(bf16[32,2,1536]{2,1,0:T(2,128)(2,1)S(1)} %reshape.102), channel_id=1, replica_groups=mesh['seq'=32,'col_0'=4,'col_1'=4] {'seq'}, dimensions={0} | all-to-all | bytes 393216 | tf_op jit(solution)/shard_map/all_to_all | solution.py:135
  487.1 0.3 reshape.103
  487.4 0.1 copy.56
  487.4 0.3 copy.57
  487.8 0.4 reshape.92
  488.1 2.3 fusion.15
  (22 shorter events, 0.2 us)
Async XLA Ops:
  6.5 167.1 %all-gather.9.cloned.1.call-start = ((), (), s32[]{:S(2)}) async-start(), calls=%async_computation.5 | async-start | bytes 6684672 | tf_op jit(solution)/shard_map/all_gather | solution.py:105
  8.8 38.8 %copy-start.1 = (bf16[48,2304]{1,0:T(8,128)(2,1)S(1)}, bf16[48,2304]{1,0:T(8,128)(2,1)}, u32[]{:S(2)}) copy-start(bf16[48,2304]{1,0:T(8,128)(2,1)} %param.11) | copy-start | bytes 663556
  8.8 38.8 %copy-start.2 = (bf16[48,768]{1,0:T(8,128)(2,1)S(1)}, bf16[48,768]{1,0:T(8,128)(2,1)}, u32[]{:S(2)}) copy-start(bf16[48,768]{1,0:T(8,128)(2,1)} %param.12) | copy-start | bytes 221188
  8.8 38.8 %copy-start.3 = (bf16[48,768]{1,0:T(8,128)(2,1)S(1)}, bf16[48,768]{1,0:T(8,128)(2,1)}, u32[]{:S(2)}) copy-start(bf16[48,768]{1,0:T(8,128)(2,1)} %param.10) | copy-start | bytes 221188
  9.8 38.6 %copy-start.4 = (s32[16,8]{0,1:T(8,128)S(1)}, s32[16,8]{0,1:T(8,128)}, u32[]{:S(2)}) copy-start(s32[16,8]{0,1:T(8,128)} %param.9) | copy-start | bytes 1540
  9.8 240.2 %all-gather.11.cloned.1.call-start = ((), (), s32[]{:S(2)}) async-start(), calls=%async_computation.6 | async-start | bytes 7864320 | tf_op jit(solution)/shard_map/all_gather | solution.py:37
  47.5 347.7 %all-gather.7.cloned.1.call-start = ((), (), s32[]{:S(2)}) async-start(), calls=%async_computation.4 | async-start | bytes 6266880 | tf_op jit(solution)/shard_map/all_gather | solution.py:20
  184.6 92.6 %all-to-all-start = ((f32[32,12,8,128]{3,2,1,0:T(8,128)}), f32[32,12,8,128]{3,2,1,0:T(8,128)}, u32[]{:S(2)}, u32[]{:S(2)}) async-start(f32[32,12,8,128]{3,2,1,0:T(8,128)} %broadcast_in_dim.16), calls=%async_computation | async-start | bytes 3145728 | tf_op jit(solution)/shard_map/all_to_all | solution.py:25
  277.8 125.9 %all-to-all-start.2 = ((bf16[16,32,3]{0,2,1:T(4,128)(2,1)}), bf16[16,32,3]{0,2,1:T(4,128)(2,1)}, u32[]{:S(2)}, u32[]{:S(2)}) async-start(bf16[16,32,3]{0,2,1:T(4,128)(2,1)} %broadcast_in_dim.23), calls=%async_computation.2 | async-start | bytes 65536 | tf_op jit(solution)/shard_map/all_to_all | solution.py:54
  286.4 0.6 copy-start
  287.2 110.0 %copy-start.5 = (f32[768]{0:T(1024)S(1)}, f32[768]{0:T(1024)}, u32[]{:S(2)}) copy-start(f32[768]{0:T(1024)} %param.13) | copy-start | bytes 9220
  403.7 55.2 %all-to-all-start.1 = ((bf16[16,32,3,192]{3,0,2,1:T(8,128)(2,1)}), bf16[16,32,3,192]{3,0,2,1:T(8,128)(2,1)S(1)}, u32[]{:S(2)}, u32[]{:S(2)}) async-start(bf16[16,32,3,192]{3,0,2,1:T(8,128)(2,1)} %reshape.88), calls=%async_computation.1 | async-start | bytes 1572864 | tf_op jit(solution)/shard_map/all_to_all | solution.py:54
Sparse Core Ops, SparseCore 0:
  10.0 163.6 all-gather.8
  175.7 74.3 all-gather.10
  252.2 142.9 all-gather.6
where the time goes:
time: 498 us; the launch traced here: 497 us
  waiting for transfers between devices  337 us (68%)
  blocking collectives  62.4 us (13%)
  starting transfers between devices  37.2 us (7%)
  local copies, waits for them, and re-layouts  28.5 us (6%)
  between operations  13.4 us (3%)
  matrix products  12.8 us (3%)
  other arithmetic  5.73 us (1%)
    all_gather x1, waiting for transfers between devices, per_device(): all_keys = lax.all_gather(keys, COL, axis=1, tiled=True)  124 us
    all_gather x1, waiting for transfers between devices, in_one_piece(): lax.all_gather(both, axis, axis=dim, tiled=True)  104 us
    all_gather x1, waiting for transfers between devices, whole_of(): filled = lax.all_gather(filled, axes[number], axis=dim, tiled=True)  48.3 us
    all_to_all x2, waiting for transfers between devices, items_in_groups(): lax.all_to_all(group, axis, split_axis=split_dim, concat_axis=concat_dim,...  41.3 us
    all_gather x1, blocking collectives, whole_of(): filled = lax.all_gather(filled, axes[number], axis=dim, tiled=True)  37.4 us
    all_to_all x1, blocking collectives, per_device(): lax.all_to_all(attended, 'seq', split_axis=0, concat_axis=1, tiled=True)  25 us
    all_to_all x2, starting transfers between devices, items_in_groups(): lax.all_to_all(group, axis, split_axis=split_dim, concat_axis=concat_dim,...  20 us
    all_to_all x1, waiting for transfers between devices, from_everyone(): lax.all_to_all(jnp.broadcast_to(array[None], (length, *array.shape)), axi...  19.1 us
  transfers between devices with their start and end apart: 6, of which 5 were waited for; matrix products, arithmetic and copies ran while one was open for 7% of the time, Pallas kernels for 0%

commit v1 on v0

--- a/solution.py
+++ b/solution.py
@@ -1,14 +1,268 @@
+import functools
 import math
 
 import jax
 import jax.numpy as jnp
 from jax import lax
+from jax.experimental import pallas as pl
+from jax.experimental.pallas import tpu as pltpu
 from jax.sharding import Mesh
 from jax.sharding import PartitionSpec as P
 
 H = 12
 DH = 64
-COL = ("col_0", "col_1")
+F32 = jnp.float32
+BF16 = jnp.bfloat16
+MESH = pl.DeviceIdType.MESH
+
+
+class Links:
+    def __init__(self, send_sem, recv_sem):
+        self.send_sem, self.recv_sem, self.count, self.started = send_sem, recv_sem, 0, []
+
+    def copy(self, src, dst, device):
+        k = self.count
+        self.count += 1
+        made = pltpu.make_async_remote_copy(
+            src_ref=src,
+            dst_ref=dst,
+            send_sem=self.send_sem.at[k],
+            recv_sem=self.recv_sem.at[k],
+            device_id=device,
+            device_id_type=MESH,
+        )
+        made.start()
+        self.started.append(made)
+        return made
+
+    def finish(self):
+        for made in self.started:
+            made.wait_send()
+
+
+class Place:
+    def __init__(self):
+        s, c = lax.axis_index("seq"), lax.axis_index("col")
+        self.x, self.zh, self.co = s // 8, (s // 2) % 4, s % 2
+        self.y, self.zl = c // 4, c % 4
+
+    def at(self, **moved):
+        g = {k: moved.get(k, getattr(self, k)) for k in ("x", "zh", "co", "y", "zl")}
+        return (g["x"] * 8 + g["zh"] * 2 + g["co"], g["y"] * 4 + g["zl"])
+
+    def group(self):
+        return self.x * 2 + self.co
+
+    def in_group(self, d):
+        g = (self.group() + d) % 8
+        return g, self.at(x=g // 2, co=g % 2)
+
+    def cousin(self):
+        return self.zh * 2 + self.zl % 2
+
+    def in_cousins(self, d):
+        e = (self.cousin() + d) % 8
+        return e, self.at(zh=e // 2, zl=(self.zl // 2) * 2 + e % 2)
+
+
+def meet(devices):
+    barrier = pltpu.get_barrier_semaphore()
+    for device in devices:
+        pl.semaphore_signal(barrier, inc=1, device_id=device, device_id_type=MESH)
+    pl.semaphore_wait(barrier, len(devices))
+
+
+def row_kernel(
+    trip, occ, out, qs, kbuf, vbuf, qbuf, lsend, lrecv, erecv, pbuf, csend, crecv, send_sem, recv_sem
+):
+    me = Place()
+    links = Links(send_sem, recv_sem)
+    along_z = [((me.zl + d) % 4, me.at(zl=(me.zl + d) % 4)) for d in range(1, 4)]
+    up, down = me.at(y=(me.y + 1) % 4), me.at(y=(me.y + 3) % 4)
+    y_up, y_down = (me.y + 1) % 4, (me.y + 3) % 4
+    cousins = []
+    for zh in range(1, 4):
+        for other in range(2):
+            cousins.append(
+                me.at(zh=(me.zh + zh) % 4, zl=(me.zl // 2) * 2 + (me.zl + other) % 2)
+            )
+    everyone = [d for _, d in along_z] + [up, down] + [me.in_group(d)[1] for d in range(1, 8)] + cousins
+
+    rows = lax.broadcasted_iota(jnp.int32, (128, 16), 0)
+    seqs = lax.broadcasted_iota(jnp.int32, (128, 16), 1)
+    spread = jnp.dot(
+        (rows // 8 == seqs).astype(BF16), occ[...].astype(F32).astype(BF16), preferred_element_type=F32
+    )
+    picked = lax.broadcasted_iota(jnp.int32, (128, 8), 0) % 8 == lax.broadcasted_iota(
+        jnp.int32, (128, 8), 1
+    )
+    live = jnp.sum(jnp.where(picked, spread, 0.0), axis=1, keepdims=True)
+    query = trip[:, :, 0:768].reshape(128, 768).astype(F32) * live
+    qs[...] = query.astype(BF16).reshape(16, 8, 768)
+
+    meet(everyone)
+
+    def share(z, first):
+        return (
+            pl.ds(pl.multiple_of((z % 2) * 8, 8), 8),
+            slice(None),
+            pl.ds(pl.multiple_of(first + (z // 2) * 384, 128), 384),
+        )
+
+    kz = [links.copy(trip.at[share(z, 768)], kbuf.at[me.y, me.zl], dev) for z, dev in along_z]
+    qz = [links.copy(qs.at[share(z, 0)], qbuf.at[me.zl], dev) for z, dev in along_z]
+    vz = [links.copy(trip.at[share(z, 1536)], vbuf.at[me.y, me.zl], dev) for z, dev in along_z]
+    kbuf[me.y, me.zl] = trip[share(me.zl, 768)]
+    vbuf[me.y, me.zl] = trip[share(me.zl, 1536)]
+    qbuf[me.zl] = qs[share(me.zl, 0)]
+
+    def around_y(buf, arrivals):
+        ups, downs = [], []
+        for d in range(4):
+            if d > 0:
+                arrivals[d - 1].wait_recv()
+            z = (me.zl + 4 - d) % 4
+            piece = buf.at[me.y, z]
+            ups.append(links.copy(piece, piece, up))
+            downs.append(links.copy(piece, piece, down))
+        return ups, downs
+
+    def relay_y(buf, ups, downs):
+        more = []
+        for d in range(2):
+            ups[d].wait_recv()
+            z = (me.zl + 4 - d) % 4
+            piece = buf.at[y_down, z]
+            more.append(links.copy(piece, piece, up))
+            downs[d + 2].wait_recv()
+            z = (me.zl + 4 - d - 2) % 4
+            piece = buf.at[y_up, z]
+            more.append(links.copy(piece, piece, down))
+        return ups[2:] + downs[:2] + more
+
+    kups, kdowns = around_y(kbuf, kz)
+    rest = relay_y(kbuf, kups, kdowns)
+    for q in qz:
+        q.wait_recv()
+    for k in rest:
+        k.wait_recv()
+
+    low = lax.broadcasted_iota(jnp.int32, (1, 128), 1) < 64
+    low_b, high_b = low.astype(F32).astype(BF16), 1.0 - low.astype(F32)
+    high_b = high_b.astype(BF16)
+
+    def add_logits(r, totals):
+        q = qbuf[:, r].reshape(32, 384)
+        k = kbuf[:, :, r].reshape(128, 384)
+        new = []
+        for p in range(3):
+            mine = q[:, 128 * p : 128 * p + 128]
+            both = jnp.concatenate([mine * low_b, mine * high_b], axis=0)
+            new.append(
+                totals[p]
+                + lax.dot_general(
+                    both,
+                    k[:, 128 * p : 128 * p + 128],
+                    (((1,), (1,)), ((), ())),
+                    preferred_element_type=F32,
+                )
+            )
+        return tuple(new)
+
+    totals = lax.fori_loop(0, 8, add_logits, (jnp.zeros((64, 128), F32),) * 3)
+    scale = 1.0 / (math.sqrt(DH) * math.sqrt(512))
+    logits = jnp.concatenate(totals, axis=0) * scale
+    for g in range(8):
+        lsend[g] = logits[24 * g : 24 * g + 24]
+    parts = []
+    for d in range(1, 8):
+        g, dev = me.in_group(d)
+        parts.append(links.copy(lsend.at[g], lrecv.at[me.group()], dev))
+    lrecv[me.group()] = lsend[me.group()]
+    vups, vdowns = around_y(vbuf, vz)
+    for part in parts:
+        part.wait_recv()
+    total = lrecv[0]
+    for g in range(1, 8):
+        total = total + lrecv[g]
+    erecv[me.cousin()] = total
+    parts = []
+    for d in range(1, 8):
+        _, dev = me.in_cousins(d)
+        slot = erecv.at[me.cousin()]
+        parts.append(links.copy(slot, slot, dev))
+    vrest = relay_y(vbuf, vups, vdowns)
+    for part in parts:
+        part.wait_recv()
+    total = erecv[0]
+    for e in range(1, 8):
+        total = total + erecv[e]
+    top = jnp.max(total, axis=1, keepdims=True)
+    grown = jnp.exp(total - top)
+    probs = (grown / jnp.sum(grown, axis=1, keepdims=True)).astype(BF16)
+    pbuf[me.group()] = probs
+    parts = []
+    for d in range(1, 8):
+        _, dev = me.in_group(d)
+        slot = pbuf.at[me.group()]
+        parts.append(links.copy(slot, slot, dev))
+    for part in vrest + parts:
+        part.wait_recv()
+    all_probs = pbuf[...].reshape(192, 128)
+
+    def context(r, carry):
+        v = vbuf[:, :, r].reshape(128, 384)
+        made = []
+        for p in range(3):
+            both = jnp.dot(
+                all_probs[64 * p : 64 * p + 64],
+                v[:, 128 * p : 128 * p + 128],
+                preferred_element_type=F32,
+            )
+            made.append(jnp.where(low, both[:32], both[32:]))
+        csend[:, r] = jnp.concatenate(made, axis=1).astype(BF16).reshape(4, 8, 384)
+        return carry
+
+    lax.fori_loop(0, 8, context, 0)
+    back = [links.copy(csend.at[z], crecv.at[me.zl], dev) for z, dev in along_z]
+    crecv[me.zl] = csend[me.zl]
+    for b in back:
+        b.wait_recv()
+    out[...] = crecv[...]
+    links.finish()
+
+
+def row_attention(trip, occ):
+    vmem = pl.BlockSpec(memory_space=pltpu.VMEM)
+    n = 9 + 24 + 21 + 3
+    return pl.pallas_call(
+        row_kernel,
+        out_shape=jax.ShapeDtypeStruct((4, 8, 8, 384), BF16),
+        in_specs=[vmem, vmem],
+        out_specs=vmem,
+        scratch_shapes=[
+            pltpu.VMEM((16, 8, 768), BF16),
+            pltpu.VMEM((4, 4, 8, 8, 384), BF16),
+            pltpu.VMEM((4, 4, 8, 8, 384), BF16),
+            pltpu.VMEM((4, 8, 8, 384), BF16),
+            pltpu.VMEM((8, 24, 128), F32),
+            pltpu.VMEM((8, 24, 128), F32),
+            pltpu.VMEM((8, 24, 128), F32),
+            pltpu.VMEM((8, 24, 128), BF16),
+            pltpu.VMEM((4, 8, 8, 384), BF16),
+            pltpu.VMEM((4, 8, 8, 384), BF16),
+            pltpu.SemaphoreType.DMA((n,)),
+            pltpu.SemaphoreType.DMA((n,)),
+        ],
+        compiler_params=pltpu.CompilerParams(
+            collective_id=1, has_side_effects=True, vmem_limit_bytes=40 * 1024 * 1024
+        ),
+        cost_estimate=pl.CostEstimate(flops=400000000, bytes_accessed=4000000, transcendentals=3000),
+        name="row_attention",
+    )(trip, occ)
+
+
+COL = ("col",)
 
 
 def in_one_piece(arrays, axis, dim, along):
@@ -85,13 +339,7 @@
     vertical_layernorm_scaling,
 ):
     protein_extent, site_extent, embedding_dimension = alignment_embedding_tensor.shape
-    total_rows = protein_extent * lax.axis_size("seq")
     live = occupancy_indicator.astype(jnp.bfloat16)
-    parts = horizontal_attention_triples.reshape(protein_extent, site_extent, 3, H, DH)
-    query = parts[:, :, 0] * live[:, :, None, None]
-    keys = parts[:, :, 1]
-    values = parts[:, :, 2]
-    scale = 1.0 / (math.sqrt(DH) * math.sqrt(total_rows))
     full_wo_row, full_qkv, full_wo_col = in_one_piece(
         (
             horizontal_attention_exit_matrix,
@@ -102,17 +350,10 @@
         0,
         1,
     )
-    all_keys = lax.all_gather(keys, COL, axis=1, tiled=True)
-    partial_value = (
-        jnp.einsum("rihd,rjhd->hij", query, all_keys, preferred_element_type=jnp.float32) * scale
-    )
-    logits = of_everyone(partial_value, "seq")
-    all_values = whole_of(values, COL, 1)
-    row_probs = jax.nn.softmax(logits, axis=-1).astype(jnp.bfloat16)
-    context = jnp.einsum(
-        "hij,rjhd->rihd", row_probs, all_values, preferred_element_type=jnp.float32
-    ).astype(jnp.bfloat16)
-    merged_attended_heads = context.reshape(protein_extent * site_extent, embedding_dimension)
+    context = row_attention(horizontal_attention_triples, occupancy_indicator)
+    merged_attended_heads = jnp.transpose(
+        context.reshape(2, protein_extent * site_extent, 384), (1, 0, 2)
+    ).reshape(protein_extent * site_extent, embedding_dimension)
     skip_connection_hidden = alignment_embedding_tensor.reshape(
         protein_extent * site_extent, embedding_dimension
     ).astype(jnp.float32) + jnp.dot(
@@ -141,7 +382,6 @@
 
 
 def solution(mesh):
-    torus = Mesh(mesh.devices.reshape(mesh.shape["seq"], 4, 4), ("seq", "col_0", "col_1"))
     in_specs = (
         P("seq", COL, None),
         P("seq", COL, None),
@@ -153,5 +393,5 @@
     )
     out_specs = P("seq", COL, None)
     return jax.shard_map(
-        per_device, mesh=torus, in_specs=in_specs, out_specs=out_specs, check_vma=False
-    )
+        per_device, mesh=mesh, in_specs=in_specs, out_specs=out_specs, check_vma=False
+    )

time: 498 us -> 278 us (0.56)
  waiting for transfers between devices: 337 us -> 116 us
  Pallas kernels: 0 us -> 64.7 us
  blocking collectives: 62.4 us -> 26.3 us
  local copies, waits for them, and re-layouts: 28.5 us -> 8.4 us
  matrix products: 12.8 us -> 7.81 us
    all_gather x2 -> x0, waiting for transfers between devices: 172 us -> none  [the longest x1 124 us: per_device(): all_keys = lax.all_gather(keys, COL, axis=1, tiled=True)]
    pallas_call x0 -> x1, Pallas kernels: none -> 64.7 us  [row_attention(): pl.pallas_call(row_kernel, out_shape=jax.ShapeDtypeStruct((4, 8, 8, 384),...]
    all_gather x1 -> x0, blocking collectives: 37.4 us -> none  [whole_of(): filled = lax.all_gather(filled, axes[number], axis=dim, tiled=True)]
    all_gather x1, waiting for transfers between devices: 104 us -> 77.6 us  [in_one_piece(): lax.all_gather(both, axis, axis=dim, tiled=True)]
    all_to_all x1 -> x0, waiting for transfers between devices: 19.1 us -> none  [from_everyone(): lax.all_to_all(jnp.broadcast_to(array[None], (length, *array.shape)), axi...]
    all_to_all x1 -> x0, starting transfers between devices: 17.1 us -> none  [from_everyone(): lax.all_to_all(jnp.broadcast_to(array[None], (length, *array.shape)), axi...]
    all_gather x2 -> x0, local copies, waits for them, and re-layouts: 15.9 us -> none  [the longest x1 7.95 us: per_device(): all_keys = lax.all_gather(keys, COL, axis=1, tiled=True)]
    all_to_all x2, starting transfers between devices: 20 us -> 33.6 us  [items_in_groups(): lax.all_to_all(group, axis, split_axis=split_dim, concat_axis=concat_dim,...]
  transfers between devices with their start and end apart: 6 -> 3, of which waited for: 5 -> 2; matrix products, arithmetic and copies ran while one was open for 7% -> 4% of each run, Pallas kernels for 0% -> 24%
where the time goes in v1:
time: 278 us; the launch traced here: 275 us
  waiting for transfers between devices  116 us (42%)
  Pallas kernels  64.7 us (23%)
  starting transfers between devices  33.6 us (12%)
  blocking collectives  26.3 us (9%)
  between operations  13.6 us (5%)
  local copies, waits for them, and re-layouts  8.4 us (3%)
  matrix products  7.81 us (3%)
  other arithmetic  4.78 us (2%)
    all_gather x1, waiting for transfers between devices, in_one_piece(): lax.all_gather(both, axis, axis=dim, tiled=True)  77.6 us
    pallas_call x1, Pallas kernels, row_attention(): pl.pallas_call(row_kernel, out_shape=jax.ShapeDtypeStruct((4, 8, 8, 384),...  64.7 us
    all_to_all x2, waiting for transfers between devices, items_in_groups(): lax.all_to_all(group, axis, split_axis=split_dim, concat_axis=concat_dim,...  38.1 us
    all_to_all x2, starting transfers between devices, items_in_groups(): lax.all_to_all(group, axis, split_axis=split_dim, concat_axis=concat_dim,...  33.6 us
    all_to_all x1, blocking collectives, per_device(): lax.all_to_all(attended, 'seq', split_axis=0, concat_axis=1, tiled=True)  26.3 us
  transfers between devices with their start and end apart: 3, of which 2 were waited for; matrix products, arithmetic and copies ran while one was open for 4% of the time, Pallas kernels for 24%

profile of v1, /device:TPU:1, one launch (start us, length us, event | category | flops | bytes accessed | tf_op | source)
XLA Modules:
  0.0 275.0 jit_solution(13707593680746506000)
XLA Ops:
  6.5 0.0 copy-start.1
  6.5 0.0 copy-start.2
  6.5 0.0 all-gather.2.cloned.1.call-start
  6.5 1.8 pad_maximum_fusion
  8.4 0.0 all-gather.2.cloned.1.call-update
  8.4 0.7 convert_element_type.32
  9.1 0.6 broadcast_in_dim.30
  9.7 19.3 %all-to-all-start.1 = ((bf16[16,32,3]{0,2,1:T(4,128)(2,1)}), bf16[16,32,3]{0,2,1:T(4,128)(2,1)}, u32[]{:S(2)}, u32[]{:S(2)}) async-start(bf16[16,32,3]{0,2,1:T(4,128)(2,1)} %broadcast_in_dim.30), calls=%async_computation.1 | async-start | bytes 65536 | tf_op jit(solution)/shard_map/all_to_all | solution.py:308
  29.0 0.8 copy.20.occ
  29.7 0.0 copy-start
  29.7 1.1 copy-done
  30.8 64.7 %row_attention.1 = bf16[4,8,8,384]{3,2,1,0:T(8,128)(2,1)S(1)} custom-call(bf16[16,8,2304]{2,1,0:T(8,128)(2,1)S(1)} %copy-done, s32[16,8]{1,0:T(8,128)S(1)} %copy.20.occ), custom_call_target="tpu_custom_call" | custom-call | flops 400000000 | bytes 4000000 | tf_op jit(solution)/shard_map/row_attention/pallas_call | solution.py:238
  95.5 0.2 copy.21
  95.7 77.6 %all-gather.2.cloned.1.call-done = bf16[768,3840]{1,0:T(8,128)(2,1)} async-done(((bf16[48,3840]{1,0:T(8,128)(2,1)}), bf16[768,3840]{1,0:T(8,128)(2,1)}) %all-gather.2.cloned.1.call-update) | async-done | bytes 5898256 | tf_op jit(solution)/shard_map/all_gather | solution.py:274
  173.3 0.0 copy-done.1
  173.3 1.7 fusion.18
  175.0 0.2 multiply_reduce_fusion
  175.2 0.0 copy-done.2
  175.2 2.7 convolution_convert_fusion
  177.9 1.0 reshape.83
  178.9 0.8 copy.22
  179.7 2.0 reshape.84
  181.8 0.0 all-to-all-done.1
  181.8 14.4 %all-to-all-start = ((bf16[16,32,3,192]{3,0,2,1:T(8,128)(2,1)}), bf16[16,32,3,192]{3,0,2,1:T(8,128)(2,1)S(1)}, u32[]{:S(2)}, u32[]{:S(2)}) async-start(bf16[16,32,3,192]{3,0,2,1:T(8,128)(2,1)} %reshape.84), calls=%async_computation | async-start | bytes 1572864 | tf_op jit(solution)/shard_map/all_to_all | solution.py:308
  196.2 0.8 compare_bitcast_fusion
  197.0 0.1 gt.26
  197.1 38.1 %all-to-all-done = bf16[16,32,3,192]{3,0,2,1:T(8,128)(2,1)S(1)} async-done(((bf16[16,32,3,192]{3,0,2,1:T(8,128)(2,1)}), bf16[16,32,3,192]{3,0,2,1:T(8,128)(2,1)S(1)}, u32[]{:S(2)}, u32[]{:S(2)}) %all-to-all-start) | async-done | bytes 589856 | tf_op jit(solution)/shard_map/all_to_all | solution.py:308
  235.2 0.1 copy.23
  235.3 0.6 fusion.12
  235.9 1.3 fusion.19
  237.2 0.5 fusion.11
  237.7 0.3 copy.29
  238.0 0.4 reshape.93
  238.3 26.3 %all_to_all.45 = bf16[32,2,1536]{2,1,0:T(2,128)(2,1)S(1)} all-to-all(bf16[32,2,1536]{2,1,0:T(2,128)(2,1)S(1)} %reshape.93), channel_id=1, replica_groups=mesh['seq'=32,'col'=16] {'seq'}, dimensions={0} | all-to-all | bytes 393216 | tf_op jit(solution)/shard_map/all_to_all | solution.py:376
  264.7 0.3 reshape.94
  265.0 0.1 copy.30
  265.0 0.3 copy.31
  265.4 0.4 reshape.88
  265.8 2.3 fusion.7
  (4 shorter events, 0.0 us)
Async XLA Ops:
  6.5 166.8 %copy-start.1 = (bf16[16,8,768]{2,1,0:T(8,128)(2,1)S(1)}, bf16[16,8,768]{2,1,0:T(8,128)(2,1)}, u32[]{:S(2)}) copy-start(bf16[16,8,768]{2,1,0:T(8,128)(2,1)} %param.7) | copy-start | bytes 589828
  6.5 168.7 %copy-start.2 = (f32[768]{0:T(1024)S(1)}, f32[768]{0:T(1024)}, u32[]{:S(2)}) copy-start(f32[768]{0:T(1024)} %param.13) | copy-start | bytes 9220
  6.5 166.7 %all-gather.2.cloned.1.call-start = ((), (), s32[]{:S(2)}) async-start(), calls=%async_computation.3 | async-start | bytes 6266880 | tf_op jit(solution)/shard_map/all_gather | solution.py:274
  9.7 172.1 %all-to-all-start.1 = ((bf16[16,32,3]{0,2,1:T(4,128)(2,1)}), bf16[16,32,3]{0,2,1:T(4,128)(2,1)}, u32[]{:S(2)}, u32[]{:S(2)}) async-start(bf16[16,32,3]{0,2,1:T(4,128)(2,1)} %broadcast_in_dim.30), calls=%async_computation.1 | async-start | bytes 65536 | tf_op jit(solution)/shard_map/all_to_all | solution.py:308
  29.7 1.1 copy-start
  181.8 53.4 %all-to-all-start = ((bf16[16,32,3,192]{3,0,2,1:T(8,128)(2,1)}), bf16[16,32,3,192]{3,0,2,1:T(8,128)(2,1)S(1)}, u32[]{:S(2)}, u32[]{:S(2)}) async-start(bf16[16,32,3,192]{3,0,2,1:T(8,128)(2,1)} %reshape.84), calls=%async_computation | async-start | bytes 1572864 | tf_op jit(solution)/shard_map/all_to_all | solution.py:308
Sparse Core Ops, SparseCore 0:
  9.4 163.7 all-gather.1

commit v2 on v1

v2 whole, which is shorter than its diff:
```python
import functools
import math

import jax
import jax.numpy as jnp
from jax import lax
from jax.experimental import pallas as pl
from jax.experimental.pallas import tpu as pltpu
from jax.sharding import Mesh
from jax.sharding import PartitionSpec as P

H = 12
DH = 64
F32 = jnp.float32
BF16 = jnp.bfloat16
MESH = pl.DeviceIdType.MESH


class Links:
    def __init__(self, send_sem, recv_sem):
        self.send_sem, self.recv_sem, self.count, self.started = send_sem, recv_sem, 0, []

    def copy(self, src, dst, device):
        k = self.count
        self.count += 1
        made = pltpu.make_async_remote_copy(
            src_ref=src,
            dst_ref=dst,
            send_sem=self.send_sem.at[k],
            recv_sem=self.recv_sem.at[k],
            device_id=device,
            device_id_type=MESH,
        )
        made.start()
        self.started.append(made)
        return made

    def finish(self):
        for made in self.started:
            made.wait_send()


class Place:
    def __init__(self):
        s, c = lax.axis_index("seq"), lax.axis_index("col")
        self.x, self.zh, self.co = s // 8, (s // 2) % 4, s % 2
        self.y, self.zl = c // 4, c % 4

    def at(self, **moved):
        g = {k: moved.get(k, getattr(self, k)) for k in ("x", "zh", "co", "y", "zl")}
        return (g["x"] * 8 + g["zh"] * 2 + g["co"], g["y"] * 4 + g["zl"])

    def group(self):
        return self.x * 2 + self.co

    def in_group(self, d):
        g = (self.group() + d) % 8
        return g, self.at(x=g // 2, co=g % 2)

    def cousin(self):
        return self.zh * 2 + self.zl % 2

    def on_ring(self, d):
        z = (4 * self.zh + self.zl + d + 16) % 16
        return self.at(zh=z // 4, zl=z % 4)

    def in_cousins(self, d):
        e = (self.cousin() + d) % 8
        return e, self.at(zh=e // 2, zl=(self.zl // 2) * 2 + e % 2)


def meet(devices):
    barrier = pltpu.get_barrier_semaphore()
    for device in devices:
        pl.semaphore_signal(barrier, inc=1, device_id=device, device_id_type=MESH)
    pl.semaphore_wait(barrier, len(devices))


class Weights:
    def __init__(self, me, links, buf, up, down):
        self.me, self.links, self.buf, self.up, self.down = me, links, buf, up, down
        self.half = pl.ds(3 * (me.x % 2), 3)
        self.y_up, self.y_down, self.y_far = (me.y + 1) % 4, (me.y + 3) % 4, (me.y + 2) % 4

    def over_z(self):
        piece = self.buf.at[self.me.y, self.me.zl, self.half]
        self.z = [self.links.copy(piece, piece, self.me.on_ring(d)) for d in (1, -1, 2)]

    def over_y(self):
        for z in self.z:
            z.wait_recv()
        piece = self.buf.at[self.me.y, :, self.half]
        self.ups = self.links.copy(piece, piece, self.up)
        self.downs = self.links.copy(piece, piece, self.down)
        self.right, self.left = self.me.at(x=(self.me.x + 1) % 4), self.me.at(x=(self.me.x + 3) % 4)
        self.xs = [self.links.copy(piece, piece, self.right)]

    def relay_y(self):
        self.ups.wait_recv()
        piece = self.buf.at[self.y_down, 0:2, self.half]
        self.far = [self.links.copy(piece, piece, self.up)]
        self.downs.wait_recv()
        piece = self.buf.at[self.y_up, 2:4, self.half]
        self.far.append(self.links.copy(piece, piece, self.down))
        piece = self.buf.at[self.y_up, :, self.half]
        self.xs.append(self.links.copy(piece, piece, self.right))
        piece = self.buf.at[self.y_down, :, self.half]
        self.xs.append(self.links.copy(piece, piece, self.left))

    def over_x(self):
        for f in self.far:
            f.wait_recv()
        piece = self.buf.at[self.y_far, :, self.half]
        self.xs.append(self.links.copy(piece, piece, self.left))

    def arrive(self):
        for x in self.xs:
            x.wait_recv()


def layer_kernel(
    emb, trip, occ, wr, wq, wc, gain, out,
    qs, kbuf, vbuf, qbuf, lsend, lrecv, erecv, pbuf, csend, crecv,
    wobuf, wqbuf, mslot, mx, resid, nsend, fbuf, nb, kc, vc, qc, asend, arecv,
    send_sem, recv_sem,
):
    me = Place()
    links = Links(send_sem, recv_sem)
    along_z = [((me.zl + d) % 4, me.at(zl=(me.zl + d) % 4)) for d in range(1, 4)]
    y_up, y_down = (me.y + 1) % 4, (me.y + 3) % 4
    up, down = me.at(y=y_up), me.at(y=y_down)
    everyone = [d for _, d in along_z] + [up, down] + [me.in_group(d)[1] for d in range(1, 8)]
    everyone += [me.on_ring(d) for d in (1, -1, 2, -2)]
    for d in range(1, 4):
        zh = (me.zh + d) % 4
        everyone.append(me.at(zh=zh, zl=(me.zl // 2) * 2 + (me.zl + 1) % 2))
        for co in range(2):
            everyone.append(me.at(zh=zh, co=(me.co + co) % 2))
            everyone.append(me.at(zh=zh, co=(me.co + co) % 2, x=3 - me.x))

    rows = lax.broadcasted_iota(jnp.int32, (128, 16), 0)
    seqs = lax.broadcasted_iota(jnp.int32, (128, 16), 1)
    spread = jnp.dot(
        (rows // 8 == seqs).astype(BF16), occ[...].astype(F32).astype(BF16), preferred_element_type=F32
    )
    picked = lax.broadcasted_iota(jnp.int32, (128, 8), 0) % 8 == lax.broadcasted_iota(
        jnp.int32, (128, 8), 1
    )
    live = jnp.sum(jnp.where(picked, spread, 0.0), axis=1, keepdims=True)
    query = trip[:, :, 0:768].reshape(128, 768).astype(F32) * live
    qs[...] = query.astype(BF16).reshape(16, 8, 768)

    lane = lax.broadcasted_iota(jnp.int32, (16, 128), 1)
    mine = (lane % 16 == lax.broadcasted_iota(jnp.int32, (16, 128), 0)) & (
        lane // 16 == me.co * 4 + me.zh
    )
    mslot[me.zh * 2 + me.co] = lax.dot_general(
        occ[...].astype(F32).astype(BF16),
        mine.astype(F32).astype(BF16),
        (((0,), (0,)), ((), ())),
        preferred_element_type=F32,
    )
    w_o = Weights(me, links, wobuf.at[me.co], up, down)
    w_q = Weights(me, links, wqbuf, up, down)
    first = (me.co == 0).astype(F32)
    both_o = wr[w_o.half].astype(F32) * first + wc[w_o.half].astype(F32) * (1.0 - first)
    wobuf[me.co, me.y, me.zl, w_o.half] = both_o.astype(BF16)
    for t in range(3):
        at = pl.ds(pl.multiple_of(768 * t + 384 * me.co, 128), 384)
        wqbuf[me.y, me.zl, w_q.half, :, 384 * t : 384 * t + 384] = wq[w_q.half, :, at]

    meet(everyone)

    def share(z, first):
        return (
            pl.ds(pl.multiple_of((z % 2) * 8, 8), 8),
            slice(None),
            pl.ds(pl.multiple_of(first + (z // 2) * 384, 128), 384),
        )

    kz = [links.copy(trip.at[share(z, 768)], kbuf.at[me.y, me.zl], dev) for z, dev in along_z]
    w_o.over_z()
    qz = [links.copy(qs.at[share(z, 0)], qbuf.at[me.zl], dev) for z, dev in along_z]
    vz = [links.copy(trip.at[share(z, 1536)], vbuf.at[me.y, me.zl], dev) for z, dev in along_z]
    w_q.over_z()
    marks = []
    slot = mslot.at[me.zh * 2 + me.co]
    for d in range(1, 8):
        e = (me.zh * 2 + me.co + d) % 8
        marks.append(links.copy(slot, slot, me.at(zh=e // 2, co=e % 2)))
    kbuf[me.y, me.zl] = trip[share(me.zl, 768)]
    vbuf[me.y, me.zl] = trip[share(me.zl, 1536)]
    qbuf[me.zl] = qs[share(me.zl, 0)]

    def around_y(buf, arrivals):
        ups, downs = [], []
        for d in range(4):
            if d > 0:
                arrivals[d - 1].wait_recv()
            z = (me.zl + 4 - d) % 4
            piece = buf.at[me.y, z]
            ups.append(links.copy(piece, piece, up))
            downs.append(links.copy(piece, piece, down))
        return ups, downs

    def relay_y(buf, ups, downs):
        more = []
        for d in range(2):
            ups[d].wait_recv()
            z = (me.zl + 4 - d) % 4
            piece = buf.at[y_down, z]
            more.append(links.copy(piece, piece, up))
            downs[d + 2].wait_recv()
            z = (me.zl + 4 - d - 2) % 4
            piece = buf.at[y_up, z]
            more.append(links.copy(piece, piece, down))
        return ups[2:] + downs[:2] + more

    kups, kdowns = around_y(kbuf, kz)
    w_o.over_y()
    rest = relay_y(kbuf, kups, kdowns)
    for mark in marks:
        mark.wait_recv()
    marked = mslot[0]
    for e in range(1, 8):
        marked = marked + mslot[e]
    mx[me.x] = marked
    marks = []
    for d in range(1, 4):
        marks.append(links.copy(mx.at[me.x], mx.at[me.x], me.at(x=(me.x + d) % 4)))
    w_o.relay_y()
    for q in qz:
        q.wait_recv()
    for k in rest:
        k.wait_recv()

    low = lax.broadcasted_iota(jnp.int32, (1, 128), 1) < 64
    low_b, high_b = low.astype(F32).astype(BF16), 1.0 - low.astype(F32)
    high_b = high_b.astype(BF16)

    def add_logits(r, totals):
        q = qbuf[:, r].reshape(32, 384)
        k = kbuf[:, :, r].reshape(128, 384)
        new = []
        for p in range(3):
            mine = q[:, 128 * p : 128 * p + 128]
            both = jnp.concatenate([mine * low_b, mine * high_b], axis=0)
            new.append(
                totals[p]
                + lax.dot_general(
                    both,
                    k[:, 128 * p : 128 * p + 128],
                    (((1,), (1,)), ((), ())),
                    preferred_element_type=F32,
                )
            )
        return tuple(new)

    totals = lax.fori_loop(0, 8, add_logits, (jnp.zeros((64, 128), F32),) * 3)
    scale = 1.0 / (math.sqrt(DH) * math.sqrt(512))
    logits = jnp.concatenate(totals, axis=0) * scale
    for g in range(8):
        lsend[g] = logits[24 * g : 24 * g + 24]
    parts = []
    for d in range(1, 8):
        g, dev = me.in_group(d)
        parts.append(links.copy(lsend.at[g], lrecv.at[me.group()], dev))
    lrecv[me.group()] = lsend[me.group()]
    vups, vdowns = around_y(vbuf, vz)
    w_o.over_x()
    for part in parts:
        part.wait_recv()
    total = lrecv[0]
    for g in range(1, 8):
        total = total + lrecv[g]
    erecv[me.cousin()] = total
    parts = []
    for d in range(1, 8):
        _, dev = me.in_cousins(d)
        slot = erecv.at[me.cousin()]
        parts.append(links.copy(slot, slot, dev))
    vrest = relay_y(vbuf, vups, vdowns)
    w_q.over_y()
    for part in parts:
        part.wait_recv()
    total = erecv[0]
    for e in range(1, 8):
        total = total + erecv[e]
    top = jnp.max(total, axis=1, keepdims=True)
    grown = jnp.exp(total - top)
    probs = (grown / jnp.sum(grown, axis=1, keepdims=True)).astype(BF16)
    pbuf[me.group()] = probs
    parts = []
    for d in range(1, 8):
        _, dev = me.in_group(d)
        slot = pbuf.at[me.group()]
        parts.append(links.copy(slot, slot, dev))
    core = me.at(co=1 - me.co)
    piece = wobuf.at[me.co, :, :, w_o.half]
    w_cores = [links.copy(piece, piece, core)]
    w_o.arrive()
    piece = wobuf.at[me.co, :, :, pl.ds(3 - 3 * (me.x % 2), 3)]
    w_cores.append(links.copy(piece, piece, core))
    w_q.relay_y()
    for part in vrest + parts:
        part.wait_recv()
    all_probs = pbuf[...].reshape(192, 128)

    def context(r, carry):
        v = vbuf[:, :, r].reshape(128, 384)
        made = []
        for p in range(3):
            both = jnp.dot(
                all_probs[64 * p : 64 * p + 64],
                v[:, 128 * p : 128 * p + 128],
                preferred_element_type=F32,
            )
            made.append(jnp.where(low, both[:32], both[32:]))
        csend[:, r] = jnp.concatenate(made, axis=1).astype(BF16).reshape(4, 8, 384)
        return carry

    lax.fori_loop(0, 8, context, 0)
    back = [links.copy(csend.at[z], crecv.at[me.zl], dev) for z, dev in along_z]
    crecv[me.zl] = csend[me.zl]
    for b in back:
        b.wait_recv()
    w_q.over_x()
    for w in w_cores:
        w.wait_recv()

    w_row = wobuf[0].reshape(768, 768)
    mixed = emb[...].reshape(128, 768).astype(F32)
    for h in range(2):
        mixed = mixed + jnp.dot(
            crecv[2 * h : 2 * h + 2].reshape(128, 384),
            w_row[384 * h : 384 * h + 384],
            preferred_element_type=F32,
        )
    resid[...] = mixed
    center = mixed - jnp.mean(mixed, axis=-1, keepdims=True)
    variance = jnp.mean(center * center, axis=-1, keepdims=True)
    normed = (center * lax.rsqrt(variance + 1e-05) * gain[...]).astype(BF16)
    above = lax.broadcasted_iota(jnp.int32, (128, 128), 0)
    along = lax.broadcasted_iota(jnp.int32, (128, 128), 1)
    turn = (along == (above % 16) * 8 + above // 16).astype(F32).astype(BF16)
    turned = jnp.dot(turn, normed, preferred_element_type=F32).astype(BF16)
    nsend[...] = turned.reshape(8, 16, 768)

    pair = me.x // 2
    step1 = {}
    for d in (2, 1, 3):
        zh = (me.zh + d) % 4
        dev = me.at(zh=zh)
        step1[d] = (
            links.copy(nsend.at[2 * zh + pair], nb.at[me.x, me.co, me.zh], dev),
            links.copy(nsend.at[2 * zh + 1 - pair], fbuf.at[me.zh], dev),
        )
    nb[me.x, me.co, me.zh] = nsend[2 * me.zh + pair]
    fbuf[me.zh] = nsend[2 * me.zh + 1 - pair]
    x_mate = (me.x // 2) * 2 + 1 - me.x % 2
    x_over = 3 - me.x
    mate, over = me.at(x=x_mate), me.at(x=x_over)
    to_mate, to_over, to_core, onward = {}, {}, [], []

    def on_arrival(d):
        if d > 0:
            for made in step1[d]:
                made.wait_recv()
        z = (me.zh + 4 - d) % 4
        piece = nb.at[me.x, me.co, z]
        to_over[d] = links.copy(fbuf.at[z], piece, over)
        to_mate[d] = links.copy(piece, piece, mate)
        to_core.append(links.copy(piece, piece, core))

    def pass_on(d):
        z = (me.zh + 4 - d) % 4
        to_over[d].wait_recv()
        piece = nb.at[x_over, me.co, z]
        onward.append(links.copy(piece, piece, mate))
        to_core.append(links.copy(piece, piece, core))
        to_mate[d].wait_recv()
        piece = nb.at[x_mate, me.co, z]
        to_core.append(links.copy(piece, piece, core))

    order = (0, 1, 3, 2)
    for n, d in enumerate(order):
        on_arrival(d)
        if n > 0:
            pass_on(order[n - 1])
    pass_on(order[-1])
    for n, d in enumerate(order):
        z = (me.zh + 4 - d) % 4
        onward[n].wait_recv()
        piece = nb.at[3 - x_mate, me.co, z]
        to_core.append(links.copy(piece, piece, core))
    w_q.arrive()
    for made in marks + to_core:
        made.wait_recv()

    tokens = nb[...].reshape(512, 768)
    w_kv = wqbuf[:, :, :, :, 384:1152].reshape(768, 768)
    keys_values = jnp.dot(tokens, w_kv, preferred_element_type=F32).astype(BF16)
    for p in range(3):
        kc[p] = keys_values[:, 128 * p : 128 * p + 128]
        vc[p] = keys_values[:, 384 + 128 * p : 512 + 128 * p]
    asking = jnp.concatenate([nb[me.x].reshape(128, 768), nb[x_over].reshape(128, 768)], axis=0)
    w_queries = wqbuf[:, :, :, :, 0:384].reshape(768, 384)
    queries = jnp.dot(asking, w_queries, preferred_element_type=F32).astype(BF16)
    for p in range(3):
        qc[p] = queries[:, 128 * p : 128 * p + 128]

    everywhere = jnp.concatenate([mx[x] for x in range(4)], axis=1)
    column = lax.broadcasted_iota(jnp.int32, (8, 512), 0) == 2 * me.zh + pair
    keep = jnp.sum(jnp.where(column, everywhere, 0.0), axis=0, keepdims=True) > 0

    def attend(p, carry):
        k, v = kc[p], vc[p]
        for b in range(4):
            q = qc[p, 64 * b : 64 * b + 64]
            both = jnp.concatenate([q * low_b, q * high_b], axis=0)
            scores = lax.dot_general(
                both, k, (((1,), (1,)), ((), ())), preferred_element_type=F32
            ) * (1.0 / math.sqrt(DH))
            scores = jnp.where(keep, scores, -1000000000.0)
            grown = jnp.exp(scores - jnp.max(scores, axis=1, keepdims=True))
            size = jnp.sum(grown, axis=1, keepdims=True)
            made = jnp.dot(grown.astype(BF16), v, preferred_element_type=F32) / size
            made = jnp.where(low, made[:64], made[64:]).astype(BF16)
            asend[b // 2, b % 2, p] = made.reshape(4, 16, 128)
        return carry

    lax.fori_loop(0, 3, attend, 0)

    mine = 2 * me.zh + pair
    backs = []
    for d in (2, 1, 3, 0):
        zh = (me.zh + d) % 4
        for far in range(2):
            for other in range(2):
                if d == far == other == 0:
                    continue
                co = (me.co + other) % 2
                x = x_over if far else me.x
                backs.append(
                    links.copy(
                        asend.at[far, co, :, zh], arecv.at[mine, me.co], me.at(x=x, zh=zh, co=co)
                    )
                )
    arecv[mine, me.co] = asend[0, me.co, :, me.zh]
    for made in backs:
        made.wait_recv()
    w_col = wobuf[1].reshape(768, 768)
    turn_back = (above == (along % 16) * 8 + along // 16).astype(F32).astype(BF16)
    attended = jnp.concatenate(
        [arecv[:, h, p].reshape(128, 128) for h in range(2) for p in range(3)], axis=1
    )
    attended = jnp.dot(turn_back, attended, preferred_element_type=F32).astype(BF16)
    out[...] = resid[...] + jnp.dot(attended, w_col, preferred_element_type=F32)
    links.finish()


def per_device(emb, trip, occ, wr, wq, wc, gain):
    vmem = pl.BlockSpec(memory_space=pltpu.VMEM)
    n = 160
    out = pl.pallas_call(
        layer_kernel,
        out_shape=jax.ShapeDtypeStruct((128, 768), F32),
        in_specs=[vmem] * 7,
        out_specs=vmem,
        scratch_shapes=[
            pltpu.VMEM((16, 8, 768), BF16),
            pltpu.VMEM((4, 4, 8, 8, 384), BF16),
            pltpu.VMEM((4, 4, 8, 8, 384), BF16),
            pltpu.VMEM((4, 8, 8, 384), BF16),
            pltpu.VMEM((8, 24, 128), F32),
            pltpu.VMEM((8, 24, 128), F32),
            pltpu.VMEM((8, 24, 128), F32),
            pltpu.VMEM((8, 24, 128), BF16),
            pltpu.VMEM((4, 8, 8, 384), BF16),
            pltpu.VMEM((4, 8, 8, 384), BF16),
            pltpu.VMEM((2, 4, 4, 6, 8, 768), BF16),
            pltpu.VMEM((4, 4, 6, 8, 1152), BF16),
            pltpu.VMEM((8, 8, 128), F32),
            pltpu.VMEM((4, 8, 128), F32),
            pltpu.VMEM((128, 768), F32),
            pltpu.VMEM((8, 16, 768), BF16),
            pltpu.VMEM((4, 16, 768), BF16),
            pltpu.VMEM((4, 2, 4, 16, 768), BF16),
            pltpu.VMEM((3, 512, 128), BF16),
            pltpu.VMEM((3, 512, 128), BF16),
            pltpu.VMEM((3, 256, 128), BF16),
            pltpu.VMEM((2, 2, 3, 4, 16, 128), BF16),
            pltpu.VMEM((8, 2, 3, 16, 128), BF16),
            pltpu.SemaphoreType.DMA((n,)),
            pltpu.SemaphoreType.DMA((n,)),
        ],
        compiler_params=pltpu.CompilerParams(
            collective_id=1, has_side_effects=True, vmem_limit_bytes=48 * 1024 * 1024
        ),
        name="msa_layer",
    )(
        emb,
        trip,
        occ,
        wr.reshape(6, 8, 768),
        wq.reshape(6, 8, 2304),
        wc.reshape(6, 8, 768),
        gain.reshape(1, 768),
    )
    return out.reshape(16, 8, 768)


def solution(mesh):
    both = P("seq", "col", None)
    return jax.shard_map(
        per_device,
        mesh=mesh,
        in_specs=(both, both, P("seq", "col"), P("col", None), P("col", None), P("col", None), P()),
        out_specs=both,
        check_vma=False,
    )
```

time: 278 us -> 109 us (0.39)
  the two profiles are of different devices: /device:TPU:1 before, /device:TPU:67 now
where the time goes in v2:
time: 109 us
  Pallas kernels  103 us (94%)
  local copies, waits for them, and re-layouts  6.21 us (6%)
    pallas_call x1, Pallas kernels, per_device(): pl.pallas_call(layer_kernel, out_shape=jax.ShapeDtypeStruct((128, 768), F...  103 us
    unnamed x16, local copies, waits for them, and re-layouts  6.21 us

profile of v2, /device:TPU:67, one launch (start us, length us, event | category | flops | bytes accessed | tf_op | source)
XLA Modules:
  0.0 108.9 jit_solution(17041342831094407208)
XLA Ops:
  0.0 0.0 copy-start.6
  0.0 0.0 copy-start.5
  0.0 0.7 copy-done.6
  0.7 0.0 copy-done.5
  0.7 0.1 copy.8.occ
  0.8 0.0 copy-start
  0.8 1.1 copy-done
  1.8 0.0 copy-start.1
  1.8 0.9 copy-done.1
  2.8 0.0 copy-start.2
  2.8 0.9 copy-done.2
  3.7 0.0 copy-start.3
  3.7 0.9 copy-done.3
  4.6 0.0 copy-start.4
  4.6 0.9 copy-done.4
  5.5 102.7 %msa_layer.1 = f32[128,768]{1,0:T(8,128)S(1)} custom-call(bf16[16,8,768]{2,1,0:T(8,128)(2,1)S(1)} %copy-done.2, bf16[16,8,2304]{2,1,0:T(8,128)(2,1)S(1)} %copy-done, s32[16,8]{1,0:T(8,128)S(1)} %copy.8.occ, bf16[6,8,768]{2,1,0:T(8,128)(2,1)S(1)} %bitcast.6, bf16[6,8,2304]{2,1,0:T(8,128)(2,1)S(1)} %bitcast.5, bf16[6,8,768]{2,1,0:T(8,128)(2,1)S(1)} %bitcast.7, ...), custom_call_target="tpu_custom_call" | custom-call | tf_op jit(solution)/shard_map/msa_layer/pallas_call | solution.py:465
  108.2 0.7 copy.10
  (1 shorter events, 0.0 us)
Async XLA Ops:
  0.0 0.7 copy-start.6
  0.0 0.7 copy-start.5
  0.8 1.1 copy-start
  1.8 0.9 copy-start.1
  2.8 0.9 copy-start.2
  3.7 0.9 copy-start.3
  4.6 0.9 copy-start.4

commit v3 on v2

v3 whole, which is shorter than its diff:
```python
import functools
import math

import jax
import jax.numpy as jnp
from jax import lax
from jax.experimental import pallas as pl
from jax.experimental.pallas import tpu as pltpu
from jax.sharding import Mesh
from jax.sharding import PartitionSpec as P

H = 12
DH = 64
F32 = jnp.float32
BF16 = jnp.bfloat16
MESH = pl.DeviceIdType.MESH


class Links:
    def __init__(self, send_sem, recv_sem):
        self.send_sem, self.recv_sem, self.count, self.started = send_sem, recv_sem, 0, []

    def copy(self, src, dst, device):
        k = self.count
        self.count += 1
        made = pltpu.make_async_remote_copy(
            src_ref=src,
            dst_ref=dst,
            send_sem=self.send_sem.at[k],
            recv_sem=self.recv_sem.at[k],
            device_id=device,
            device_id_type=MESH,
        )
        made.start()
        self.started.append(made)
        return made

    def finish(self):
        for made in self.started:
            made.wait_send()


class Place:
    def __init__(self):
        s, c = lax.axis_index("seq"), lax.axis_index("col")
        self.x, self.zh, self.co = s // 8, (s // 2) % 4, s % 2
        self.y, self.zl = c // 4, c % 4

    def at(self, **moved):
        g = {k: moved.get(k, getattr(self, k)) for k in ("x", "zh", "co", "y", "zl")}
        return (g["x"] * 8 + g["zh"] * 2 + g["co"], g["y"] * 4 + g["zl"])

    def group(self):
        return self.x * 4 + self.co * 2 + self.zl % 2

    def in_group(self, d):
        g = (self.group() + d) % 16
        return g, self.at(x=g // 4, co=(g // 2) % 2, zl=(self.zl // 2) * 2 + g % 2)

    def on_ring(self, d):
        z = (4 * self.zh + self.zl + d + 16) % 16
        return self.at(zh=z // 4, zl=z % 4)


def meet(devices):
    barrier = pltpu.get_barrier_semaphore()
    for device in devices:
        pl.semaphore_signal(barrier, inc=1, device_id=device, device_id_type=MESH)
    pl.semaphore_wait(barrier, len(devices))


class Weights:
    def __init__(self, me, links, buf, rows, up, down):
        self.me, self.links, self.buf, self.rows, self.up, self.down = me, links, buf, rows, up, down
        self.y_up, self.y_down, self.y_far = (me.y + 1) % 4, (me.y + 3) % 4, (me.y + 2) % 4
        self.right, self.left = me.at(x=(me.x + 1) % 4), me.at(x=(me.x + 3) % 4)
        self.xs = []

    def send(self, piece, device):
        return self.links.copy(piece, piece, device)

    def over_z(self):
        piece = self.buf.at[self.me.y, self.me.zl, self.rows]
        self.z = [self.send(piece, self.me.on_ring(d)) for d in (1, -1, 2)]

    def over_y(self):
        for z in self.z:
            z.wait_recv()
        piece = self.buf.at[self.me.y, :, self.rows]
        self.ups = self.send(piece, self.up)
        self.downs = self.send(piece, self.down)

    def relay_y(self):
        self.ups.wait_recv()
        self.far = [self.send(self.buf.at[self.y_down, 0:2, self.rows], self.up)]
        self.downs.wait_recv()
        self.far.append(self.send(self.buf.at[self.y_up, 2:4, self.rows], self.down))

    def near_x(self):
        for y, device in ((self.me.y, self.right), (self.y_up, self.right), (self.y_down, self.left)):
            self.xs.append(self.send(self.buf.at[y, :, self.rows], device))

    def far_y(self):
        for f in self.far:
            f.wait_recv()

    def far_x(self):
        self.xs.append(self.send(self.buf.at[self.y_far, :, self.rows], self.left))

    def arrive(self):
        for x in self.xs:
            x.wait_recv()

    def to_core(self, core, rows):
        return self.send(self.buf.at[:, :, rows], core)


def layer_kernel(
    emb, trip, occ, wr, wq, wc, gain, out,
    qraw, qs, kbuf, vbuf, qbuf, lsend, lrecv, erecv, pbuf, csend, crecv,
    wrbuf, wcbuf, wqbuf, mslot, mx, resid, nsend, xr, nb, kc, vc, qc, asend, arecv,
    occ_in, emb_in, gain_in, send_sem, recv_sem, load_sem,
):
    me = Place()
    links = Links(send_sem, recv_sem)
    along_z = [((me.zl + d) % 4, me.at(zl=(me.zl + d) % 4)) for d in range(1, 4)]
    y_up, y_down = (me.y + 1) % 4, (me.y + 3) % 4
    up, down = me.at(y=y_up), me.at(y=y_down)
    everyone = [d for _, d in along_z] + [up, down] + [me.in_group(d)[1] for d in range(1, 16)]
    everyone += [me.on_ring(d) for d in (1, -1, 2, -2)]
    for d in range(1, 4):
        zh = (me.zh + d) % 4
        everyone.append(me.at(zh=zh, co=1 - me.co))
        for e in range(4):
            everyone.append(me.at(zh=zh, x=(me.x + e) % 4))

    loads = []

    def load(src, dst):
        made = pltpu.make_async_copy(src, dst, load_sem.at[len(loads)])
        made.start()
        loads.append(made)
        return made

    def share(z, first):
        return (
            pl.ds(pl.multiple_of((z % 2) * 8, 8), 8),
            slice(None),
            pl.ds(pl.multiple_of(first + (z // 2) * 384, 128), 384),
        )

    half, other_half = pl.ds(3 * (me.x % 2), 3), pl.ds(3 - 3 * (me.x % 2), 3)
    w_r = Weights(me, links, wrbuf.at[me.co], half, up, down)
    w_c = Weights(me, links, wcbuf.at[me.co], slice(None), up, down)
    core_half = pl.ds(3 * me.co, 3)
    w_q = Weights(me, links, wqbuf, core_half, up, down)
    core = me.at(co=1 - me.co)
    half_lanes = pl.ds(pl.multiple_of(384 * me.co, 128), 384)
    q_loads = [load(trip.at[:, :, 0:768], qraw), load(occ, occ_in)]
    k_load = load(trip.at[share(me.zl, 768)], kbuf.at[me.y, me.zl])
    w_loads = [
        load(wr.at[half, :, half_lanes], wrbuf.at[me.co, me.y, me.zl, half]),
        load(wc.at[:, :, half_lanes], wcbuf.at[me.co, me.y, me.zl]),
    ]
    for t in range(3):
        at = pl.ds(pl.multiple_of(768 * t + 384 * (me.x % 2), 128), 384)
        w_loads.append(
            load(
                wq.at[core_half, :, at],
                wqbuf.at[me.y, me.zl, core_half, :, 384 * t : 384 * t + 384],
            )
        )
    v_load = load(trip.at[share(me.zl, 1536)], vbuf.at[me.y, me.zl])
    last_loads = [load(emb, emb_in), load(gain, gain_in)]

    meet(everyone)

    kz = [links.copy(trip.at[share(z, 768)], kbuf.at[me.y, me.zl], dev) for z, dev in along_z]
    k_load.wait()
    piece = kbuf.at[me.y, me.zl]
    kups, kdowns = [links.copy(piece, piece, up)], [links.copy(piece, piece, down)]

    for made in q_loads:
        made.wait()
    rows = lax.broadcasted_iota(jnp.int32, (128, 16), 0)
    seqs = lax.broadcasted_iota(jnp.int32, (128, 16), 1)
    occupied = occ_in[...].astype(F32).astype(BF16)
    spread = lax.dot_general(
        (rows // 8 == seqs).astype(F32).astype(BF16),
        occupied,
        (((1,), (1,)), ((), ())),
        preferred_element_type=F32,
    )
    picked = lax.broadcasted_iota(jnp.int32, (128, 8), 0) % 8 == lax.broadcasted_iota(
        jnp.int32, (128, 8), 1
    )
    live = jnp.sum(jnp.where(picked, spread, 0.0), axis=1, keepdims=True)
    query = qraw[...].reshape(128, 768).astype(F32) * live
    qs[...] = query.astype(BF16).reshape(16, 8, 768)
    qz = [links.copy(qs.at[share(z, 0)], qbuf.at[me.zl], dev) for z, dev in along_z]
    for made in w_loads:
        made.wait()
    w_r.over_z()
    qbuf[me.zl] = qs[share(me.zl, 0)]

    lane = lax.broadcasted_iota(jnp.int32, (16, 128), 1)
    mine = (lane % 16 == lax.broadcasted_iota(jnp.int32, (16, 128), 0)) & (
        lane // 16 == me.co * 4 + me.zh
    )
    mslot[me.zh * 2 + me.co] = jnp.dot(
        occupied, mine.astype(F32).astype(BF16), preferred_element_type=F32
    )
    marks = []
    slot = mslot.at[me.zh * 2 + me.co]
    for d in range(1, 8):
        e = (me.zh * 2 + me.co + d) % 8
        marks.append(links.copy(slot, slot, me.at(zh=e // 2, co=e % 2)))

    def around_y(buf, arrivals, ups, downs):
        for d in range(len(ups), 4):
            if d > 0:
                arrivals[d - 1].wait_recv()
            piece = buf.at[me.y, (me.zl + 4 - d) % 4]
            ups.append(links.copy(piece, piece, up))
            downs.append(links.copy(piece, piece, down))

    def relay_y(buf, ups, downs):
        more = []
        for d in range(2):
            ups[d].wait_recv()
            z = (me.zl + 4 - d) % 4
            piece = buf.at[y_down, z]
            more.append(links.copy(piece, piece, up))
            downs[d + 2].wait_recv()
            z = (me.zl + 4 - d - 2) % 4
            piece = buf.at[y_up, z]
            more.append(links.copy(piece, piece, down))
        return ups[2:] + downs[:2] + more

    around_y(kbuf, kz, kups, kdowns)
    rest = relay_y(kbuf, kups, kdowns)
    w_r.over_y()
    for q in qz:
        q.wait_recv()
    vz = [links.copy(trip.at[share(z, 1536)], vbuf.at[me.y, me.zl], dev) for z, dev in along_z]
    for k in rest:
        k.wait_recv()

    low = lax.broadcasted_iota(jnp.int32, (1, 128), 1) < 64
    low_b, high_b = low.astype(F32).astype(BF16), 1.0 - low.astype(F32)
    high_b = high_b.astype(BF16)

    def add_logits(r, totals):
        q = qbuf[:, r].reshape(32, 384)
        k = kbuf[:, :, r].reshape(128, 384)
        new = []
        for p in range(3):
            mine = q[:, 128 * p : 128 * p + 128]
            both = jnp.concatenate([mine * low_b, mine * high_b], axis=0)
            new.append(
                totals[p]
                + lax.dot_general(
                    both,
                    k[:, 128 * p : 128 * p + 128],
                    (((1,), (1,)), ((), ())),
                    preferred_element_type=F32,
                )
            )
        return tuple(new)

    totals = lax.fori_loop(0, 8, add_logits, (jnp.zeros((64, 128), F32),) * 3)
    scale = 1.0 / (math.sqrt(DH) * math.sqrt(512))
    logits = jnp.concatenate(totals, axis=0) * scale
    for g in range(16):
        lsend[g] = logits[12 * g : 12 * g + 12]
    parts = []
    for d in range(1, 16):
        g, dev = me.in_group(d)
        parts.append(links.copy(lsend.at[g], lrecv.at[me.group()], dev))
    lrecv[me.group()] = lsend[me.group()]
    w_q.over_z()
    w_c.over_z()
    for part in parts:
        part.wait_recv()
    total = lrecv[0]
    for g in range(1, 16):
        total = total + lrecv[g]
    erecv[me.zh] = total
    parts = []
    for d in (2, 1, 3):
        slot = erecv.at[me.zh]
        parts.append(links.copy(slot, slot, me.at(zh=(me.zh + d) % 4)))
    v_load.wait()
    vups, vdowns = [], []
    around_y(vbuf, vz, vups, vdowns)
    w_r.relay_y()
    w_r.near_x()
    for part in parts:
        part.wait_recv()
    total = erecv[0]
    for e in range(1, 4):
        total = total + erecv[e]
    top = jnp.max(total, axis=1, keepdims=True)
    grown = jnp.exp(total - top)
    pbuf[me.group()] = grown / jnp.sum(grown, axis=1, keepdims=True)
    parts = []
    for d in range(1, 16):
        _, dev = me.in_group(d)
        slot = pbuf.at[me.group()]
        parts.append(links.copy(slot, slot, dev))
    vrest = relay_y(vbuf, vups, vdowns)
    w_r.far_y()
    w_r.far_x()
    w_cores = [w_r.to_core(core, half)]
    w_q.over_y()
    for mark in marks:
        mark.wait_recv()
    marked = mslot[0]
    for e in range(1, 8):
        marked = marked + mslot[e]
    mx[me.x] = marked
    marks = []
    for d in range(1, 4):
        marks.append(links.copy(mx.at[me.x], mx.at[me.x], me.at(x=(me.x + d) % 4)))
    for part in vrest + parts:
        part.wait_recv()
    all_probs = jnp.concatenate([pbuf[g] for g in range(16)], axis=0).astype(BF16)

    def context(r, carry):
        v = vbuf[:, :, r].reshape(128, 384)
        made = []
        for p in range(3):
            both = jnp.dot(
                all_probs[64 * p : 64 * p + 64],
                v[:, 128 * p : 128 * p + 128],
                preferred_element_type=F32,
            )
            made.append(jnp.where(low, both[:32], both[32:]))
        csend[:, r] = jnp.concatenate(made, axis=1).astype(BF16).reshape(4, 8, 384)
        return carry

    lax.fori_loop(0, 8, context, 0)
    back = [links.copy(csend.at[z], crecv.at[me.zl], dev) for z, dev in along_z]
    crecv[me.zl] = csend[me.zl]
    w_r.arrive()
    w_cores.append(w_r.to_core(core, other_half))
    w_q.relay_y()
    w_c.over_y()
    for made in last_loads:
        made.wait()
    for made in back + w_cores:
        made.wait_recv()

    mixed = emb_in[...].reshape(128, 768).astype(F32)
    for h in range(2):
        context_half = crecv[2 * h : 2 * h + 2].reshape(128, 384)
        made = [
            jnp.dot(
                context_half,
                wrbuf[n, 2 * h : 2 * h + 2].reshape(384, 384),
                preferred_element_type=F32,
            )
            for n in range(2)
        ]
        mixed = mixed + jnp.concatenate(made, axis=1)
    resid[...] = mixed
    center = mixed - jnp.mean(mixed, axis=-1, keepdims=True)
    variance = jnp.mean(center * center, axis=-1, keepdims=True)
    normed = (center * lax.rsqrt(variance + 1e-05) * gain_in[...].reshape(1, 768)).astype(BF16)
    above = lax.broadcasted_iota(jnp.int32, (128, 128), 0)
    along = lax.broadcasted_iota(jnp.int32, (128, 128), 1)
    column_at = above // 16 % 4 * 2 + above // 64
    turn = (along == (above % 16) * 8 + column_at).astype(F32).astype(BF16)
    turned = jnp.dot(turn, normed, preferred_element_type=F32).astype(BF16)
    nsend[...] = turned.reshape(2, 4, 16, 768)

    pair = me.x // 2
    x_mate = (me.x // 2) * 2 + 1 - me.x % 2
    x_over = 3 - me.x
    mate, over = me.at(x=x_mate), me.at(x=x_over)
    crossed = links.copy(nsend.at[1 - pair], xr, over)
    order = (2, 1, 3)

    def there(d):
        return (me.zh + d) % 4

    own = [
        links.copy(nsend.at[pair, there(d)], nb.at[me.x, me.co, me.zh], me.at(zh=there(d)))
        for d in order
    ]
    nb[me.x, me.co, me.zh] = nsend[pair, me.zh]
    crossed.wait_recv()
    far = [
        links.copy(xr.at[there(d)], nb.at[x_over, me.co, me.zh], me.at(zh=there(d))) for d in order
    ]
    nb[x_over, me.co, me.zh] = xr[me.zh]
    w_q.far_y()
    w_q_core = w_q.to_core(core, core_half)
    w_c.relay_y()
    for made in own:
        made.wait_recv()
    piece = nb.at[me.x, me.co]
    to_mate = [links.copy(piece, piece, mate)]
    to_core = [links.copy(piece, piece, core)]
    for n, d in ((None, 0), (1, 1), (2, 3), (0, 2)):
        if n is not None:
            far[n].wait_recv()
        piece = nb.at[x_over, me.co, (me.zh + 4 - d) % 4]
        to_mate.append(links.copy(piece, piece, mate))
        to_core.append(links.copy(piece, piece, core))
    to_mate[0].wait_recv()
    piece = nb.at[x_mate, me.co]
    to_core.append(links.copy(piece, piece, core))
    for n, d in enumerate((0, 1, 3, 2)):
        to_mate[n + 1].wait_recv()
        piece = nb.at[3 - x_mate, me.co, (me.zh + 4 - d) % 4]
        to_core.append(links.copy(piece, piece, core))
    w_c.far_y()
    w_c_core = w_c.to_core(core, slice(None))
    w_q_core.wait_recv()
    for made in marks + to_core:
        made.wait_recv()

    tokens = nb[...].reshape(512, 768)
    w_kv = wqbuf[:, :, :, :, 384:1152].reshape(768, 768)
    keys_values = jnp.dot(tokens, w_kv, preferred_element_type=F32).astype(BF16)
    for p in range(3):
        kc[p] = keys_values[:, 128 * p : 128 * p + 128]
        vc[p] = keys_values[:, 384 + 128 * p : 512 + 128 * p]
    asking = nb[:, me.co].reshape(256, 768)
    w_queries = wqbuf[:, :, :, :, 0:384].reshape(768, 384)
    queries = jnp.dot(asking, w_queries, preferred_element_type=F32).astype(BF16)
    for p in range(3):
        qc[p] = queries[:, 128 * p : 128 * p + 128]

    everywhere = jnp.concatenate([mx[x] for x in range(4)], axis=1)
    column = lax.broadcasted_iota(jnp.int32, (8, 512), 0) == 2 * me.zh + pair
    keep = jnp.sum(jnp.where(column, everywhere, 0.0), axis=0, keepdims=True) > 0

    def attend(p, carry):
        k, v = kc[p], vc[p]
        for b in range(4):
            q = qc[p, 64 * b : 64 * b + 64]
            both = jnp.concatenate([q * low_b, q * high_b], axis=0)
            scores = lax.dot_general(
                both, k, (((1,), (1,)), ((), ())), preferred_element_type=F32
            ) * (1.0 / math.sqrt(DH))
            scores = jnp.where(keep, scores, -1000000000.0)
            grown = jnp.exp(scores - jnp.max(scores, axis=1, keepdims=True))
            size = jnp.sum(grown, axis=1, keepdims=True)
            made = jnp.dot(grown.astype(BF16), v, preferred_element_type=F32) / size
            made = jnp.where(low, made[:64], made[64:]).astype(BF16)
            asend[b, p] = made.reshape(4, 16, 128)
        return carry

    lax.fori_loop(0, 3, attend, 0)

    mine = 2 * me.zh + pair
    backs = []
    for d in (2, 1, 3, 0):
        zh = (me.zh + d) % 4
        for e in (2, 1, 3, 0):
            if d == e == 0:
                continue
            x = (me.x + e) % 4
            backs.append(
                links.copy(asend.at[x, :, zh], arecv.at[mine, me.x % 2], me.at(x=x, zh=zh))
            )
    arecv[mine, me.x % 2] = asend[me.x, :, me.zh]
    for made in backs:
        made.wait_recv()
    w_c_core.wait_recv()
    turn_back = (above == (along % 16) * 8 + along // 16).astype(F32).astype(BF16)
    attended = jnp.concatenate(
        [arecv[:, h, p].reshape(128, 128) for h in range(2) for p in range(3)], axis=1
    )
    attended = jnp.dot(turn_back, attended, preferred_element_type=F32).astype(BF16)
    for n in range(2):
        out[:, 384 * n : 384 * n + 384] = resid[:, 384 * n : 384 * n + 384] + jnp.dot(
            attended, wcbuf[n].reshape(768, 384), preferred_element_type=F32
        )
    links.finish()


def per_device(emb, trip, occ, wr, wq, wc, gain):
    vmem = pl.BlockSpec(memory_space=pltpu.VMEM)
    n = 160
    out = pl.pallas_call(
        layer_kernel,
        out_shape=jax.ShapeDtypeStruct((128, 768), F32),
        in_specs=[pl.BlockSpec(memory_space=pl.ANY)] * 7,
        out_specs=vmem,
        scratch_shapes=[
            pltpu.VMEM((16, 8, 768), BF16),
            pltpu.VMEM((16, 8, 768), BF16),
            pltpu.VMEM((4, 4, 8, 8, 384), BF16),
            pltpu.VMEM((4, 4, 8, 8, 384), BF16),
            pltpu.VMEM((4, 8, 8, 384), BF16),
            pltpu.VMEM((16, 12, 128), F32),
            pltpu.VMEM((16, 12, 128), F32),
            pltpu.VMEM((4, 12, 128), F32),
            pltpu.VMEM((16, 12, 128), F32),
            pltpu.VMEM((4, 8, 8, 384), BF16),
            pltpu.VMEM((4, 8, 8, 384), BF16),
            pltpu.VMEM((2, 4, 4, 6, 8, 384), BF16),
            pltpu.VMEM((2, 4, 4, 6, 8, 384), BF16),
            pltpu.VMEM((4, 4, 6, 8, 1152), BF16),
            pltpu.VMEM((8, 8, 128), F32),
            pltpu.VMEM((4, 8, 128), F32),
            pltpu.VMEM((128, 768), F32),
            pltpu.VMEM((2, 4, 16, 768), BF16),
            pltpu.VMEM((4, 16, 768), BF16),
            pltpu.VMEM((4, 2, 4, 16, 768), BF16),
            pltpu.VMEM((3, 512, 128), BF16),
            pltpu.VMEM((3, 512, 128), BF16),
            pltpu.VMEM((3, 256, 128), BF16),
            pltpu.VMEM((4, 3, 4, 16, 128), BF16),
            pltpu.VMEM((8, 2, 3, 16, 128), BF16),
            pltpu.VMEM((8, 16), jnp.int32),
            pltpu.VMEM((16, 8, 768), BF16),
            pltpu.VMEM((768,), F32),
            pltpu.SemaphoreType.DMA((n,)),
            pltpu.SemaphoreType.DMA((n,)),
            pltpu.SemaphoreType.DMA((12,)),
        ],
        compiler_params=pltpu.CompilerParams(
            collective_id=1, has_side_effects=True, vmem_limit_bytes=56 * 1024 * 1024
        ),
        name="msa_layer",
    )(
        emb,
        trip,
        occ.T,
        wr.reshape(6, 8, 768),
        wq.reshape(6, 8, 2304),
        wc.reshape(6, 8, 768),
        gain,
    )
    return out.reshape(16, 8, 768)


def solution(mesh):
    both = P("seq", "col", None)
    return jax.shard_map(
        per_device,
        mesh=mesh,
        in_specs=(both, both, P("seq", "col"), P("col", None), P("col", None), P("col", None), P()),
        out_specs=both,
        check_vma=False,
    )
```

time: 109 us -> 99.8 us (0.916)
  the two profiles are of different devices: /device:TPU:67 before, /device:TPU:1 now
where the time goes in v3:
time: 99.8 us; the launch traced here: 99.6 us
  Pallas kernels  97.9 us (98%)
  local copies, waits for them, and re-layouts  1.77 us (2%)
    pallas_call x1, Pallas kernels, per_device(): pl.pallas_call(layer_kernel, out_shape=jax.ShapeDtypeStruct((128, 768), F...  97.9 us

profile of v3, /device:TPU:1, one launch (start us, length us, event | category | flops | bytes accessed | tf_op | source)
XLA Modules:
  0.0 99.6 jit_solution(16146174701554888580)
XLA Ops:
  0.0 97.9 %msa_layer.1 = f32[128,768]{1,0:T(8,128)} custom-call(bf16[16,8,768]{2,1,0:T(8,128)(2,1)} %emb.1, bf16[16,8,2304]{2,1,0:T(8,128)(2,1)} %trip.1, s32[8,16]{1,0:T(8,128)} %bitcast.9, bf16[6,8,768]{2,1,0:T(8,128)(2,1)} %bitcast.7, bf16[6,8,2304]{2,1,0:T(8,128)(2,1)} %bitcast.6, bf16[6,8,768]{2,1,0:T(8,128)(2,1)} %bitcast.8, f32[768]{0:T(1024)} %gain.1), custom_call_target="tpu_custom_call" | custom-call | tf_op jit(solution)/shard_map/msa_layer/pallas_call | solution.py:488
  97.9 1.8 %copy.9 = f32[16,8,768]{2,1,0:T(8,128)} copy(f32[16,8,768]{2,1,0:T(8,128)} %bitcast.5) | data formatting | bytes 786432

commit v4 on v3

--- a/solution.py
+++ b/solution.py
@@ -14,6 +14,29 @@
 F32 = jnp.float32
 BF16 = jnp.bfloat16
 MESH = pl.DeviceIdType.MESH
+
+
+class Group:
+    def __init__(self, links, whole):
+        self.links, self.whole, self.k = links, whole, links.count
+        links.count += 1
+        links.started.append(self)
+
+    def add(self, src, dst, device):
+        pltpu.make_async_remote_copy(
+            src_ref=src,
+            dst_ref=dst,
+            send_sem=self.links.send_sem.at[self.k],
+            recv_sem=self.links.recv_sem.at[self.k],
+            device_id=device,
+            device_id_type=MESH,
+        ).start()
+
+    def wait_recv(self):
+        pltpu.make_async_copy(self.whole, self.whole, self.links.recv_sem.at[self.k]).wait()
+
+    def wait_send(self):
+        pltpu.make_async_copy(self.whole, self.whole, self.links.send_sem.at[self.k]).wait()
 
 
 class Links:
@@ -57,10 +80,6 @@
         g = (self.group() + d) % 16
         return g, self.at(x=g // 4, co=(g // 2) % 2, zl=(self.zl // 2) * 2 + g % 2)
 
-    def on_ring(self, d):
-        z = (4 * self.zh + self.zl + d + 16) % 16
-        return self.at(zh=z // 4, zl=z % 4)
-
 
 def meet(devices):
     barrier = pltpu.get_barrier_semaphore()
@@ -74,45 +93,65 @@
         self.me, self.links, self.buf, self.rows, self.up, self.down = me, links, buf, rows, up, down
         self.y_up, self.y_down, self.y_far = (me.y + 1) % 4, (me.y + 3) % 4, (me.y + 2) % 4
         self.right, self.left = me.at(x=(me.x + 1) % 4), me.at(x=(me.x + 3) % 4)
-        self.xs = []
 
     def send(self, piece, device):
         return self.links.copy(piece, piece, device)
 
     def over_z(self):
         piece = self.buf.at[self.me.y, self.me.zl, self.rows]
-        self.z = [self.send(piece, self.me.on_ring(d)) for d in (1, -1, 2)]
+        self.z = Group(self.links, self.buf.at[0, 0:3, self.rows])
+        for d in (1, 3, 2):
+            self.z.add(piece, piece, self.me.at(zl=(self.me.zl + d) % 4))
 
     def over_y(self):
-        for z in self.z:
-            z.wait_recv()
+        self.z.wait_recv()
         piece = self.buf.at[self.me.y, :, self.rows]
         self.ups = self.send(piece, self.up)
         self.downs = self.send(piece, self.down)
 
     def relay_y(self):
+        self.far = Group(self.links, self.buf.at[0, :, self.rows])
         self.ups.wait_recv()
-        self.far = [self.send(self.buf.at[self.y_down, 0:2, self.rows], self.up)]
+        piece = self.buf.at[self.y_down, 0:2, self.rows]
+        self.far.add(piece, piece, self.up)
         self.downs.wait_recv()
-        self.far.append(self.send(self.buf.at[self.y_up, 2:4, self.rows], self.down))
+        piece = self.buf.at[self.y_up, 2:4, self.rows]
+        self.far.add(piece, piece, self.down)
 
     def near_x(self):
+        self.xs = Group(self.links, self.buf.at[:, :, self.rows])
         for y, device in ((self.me.y, self.right), (self.y_up, self.right), (self.y_down, self.left)):
-            self.xs.append(self.send(self.buf.at[y, :, self.rows], device))
+            piece = self.buf.at[y, :, self.rows]
+            self.xs.add(piece, piece, device)
 
     def far_y(self):
-        for f in self.far:
-            f.wait_recv()
+        self.far.wait_recv()
 
     def far_x(self):
-        self.xs.append(self.send(self.buf.at[self.y_far, :, self.rows], self.left))
+        piece = self.buf.at[self.y_far, :, self.rows]
+        self.xs.add(piece, piece, self.left)
 
     def arrive(self):
-        for x in self.xs:
-            x.wait_recv()
+        self.xs.wait_recv()
 
     def to_core(self, core, rows):
         return self.send(self.buf.at[:, :, rows], core)
+
+
+class Ring:
+    def __init__(self, me, links, buf, up, down):
+        self.me, self.links, self.buf, self.up, self.down = me, links, buf, up, down
+        self.ups, self.downs = {}, {}
+        self.rest = Group(links, buf.at[0:2])
+
+    def send(self, d):
+        piece = self.buf.at[self.me.y, (self.me.zl + 4 - d) % 4]
+        if d < 2:
+            self.ups[d] = self.links.copy(piece, piece, self.up)
+            self.rest.add(piece, piece, self.down)
+        else:
+            self.rest.add(piece, piece, self.up)
+            self.downs[d] = self.links.copy(piece, piece, self.down)
 
 
 def layer_kernel(
@@ -127,10 +166,8 @@
     y_up, y_down = (me.y + 1) % 4, (me.y + 3) % 4
     up, down = me.at(y=y_up), me.at(y=y_down)
     everyone = [d for _, d in along_z] + [up, down] + [me.in_group(d)[1] for d in range(1, 16)]
-    everyone += [me.on_ring(d) for d in (1, -1, 2, -2)]
     for d in range(1, 4):
         zh = (me.zh + d) % 4
-        everyone.append(me.at(zh=zh, co=1 - me.co))
         for e in range(4):
             everyone.append(me.at(zh=zh, x=(me.x + e) % 4))
 
@@ -177,8 +214,8 @@
 
     kz = [links.copy(trip.at[share(z, 768)], kbuf.at[me.y, me.zl], dev) for z, dev in along_z]
     k_load.wait()
-    piece = kbuf.at[me.y, me.zl]
-    kups, kdowns = [links.copy(piece, piece, up)], [links.copy(piece, piece, down)]
+    kring = Ring(me, links, kbuf, up, down)
+    kring.send(0)
 
     for made in q_loads:
         made.wait()
@@ -197,7 +234,9 @@
     live = jnp.sum(jnp.where(picked, spread, 0.0), axis=1, keepdims=True)
     query = qraw[...].reshape(128, 768).astype(F32) * live
     qs[...] = query.astype(BF16).reshape(16, 8, 768)
-    qz = [links.copy(qs.at[share(z, 0)], qbuf.at[me.zl], dev) for z, dev in along_z]
+    qz = Group(links, qbuf.at[0:3])
+    for z, dev in along_z:
+        qz.add(qs.at[share(z, 0)], qbuf.at[me.zl], dev)
     for made in w_loads:
         made.wait()
     w_r.over_z()
@@ -207,42 +246,33 @@
     mine = (lane % 16 == lax.broadcasted_iota(jnp.int32, (16, 128), 0)) & (
         lane // 16 == me.co * 4 + me.zh
     )
-    mslot[me.zh * 2 + me.co] = jnp.dot(
+    mslot[me.zh] = jnp.dot(
         occupied, mine.astype(F32).astype(BF16), preferred_element_type=F32
     )
-    marks = []
-    slot = mslot.at[me.zh * 2 + me.co]
-    for d in range(1, 8):
-        e = (me.zh * 2 + me.co + d) % 8
-        marks.append(links.copy(slot, slot, me.at(zh=e // 2, co=e % 2)))
-
-    def around_y(buf, arrivals, ups, downs):
-        for d in range(len(ups), 4):
-            if d > 0:
-                arrivals[d - 1].wait_recv()
-            piece = buf.at[me.y, (me.zl + 4 - d) % 4]
-            ups.append(links.copy(piece, piece, up))
-            downs.append(links.copy(piece, piece, down))
-
-    def relay_y(buf, ups, downs):
-        more = []
+    marks = Group(links, mslot.at[0:3])
+    for d in range(1, 4):
+        marks.add(mslot.at[me.zh], mslot.at[me.zh], me.at(zh=(me.zh + d) % 4))
+
+    def around_y(buf, arrivals, ring):
+        for d in range(1, 4):
+            arrivals[d - 1].wait_recv()
+            ring.send(d)
+
+    def relay_y(buf, ring):
         for d in range(2):
-            ups[d].wait_recv()
-            z = (me.zl + 4 - d) % 4
-            piece = buf.at[y_down, z]
-            more.append(links.copy(piece, piece, up))
-            downs[d + 2].wait_recv()
-            z = (me.zl + 4 - d - 2) % 4
-            piece = buf.at[y_up, z]
-            more.append(links.copy(piece, piece, down))
-        return ups[2:] + downs[:2] + more
-
-    around_y(kbuf, kz, kups, kdowns)
-    rest = relay_y(kbuf, kups, kdowns)
+            ring.ups[d].wait_recv()
+            piece = buf.at[y_down, (me.zl + 4 - d) % 4]
+            ring.rest.add(piece, piece, up)
+            ring.downs[d + 2].wait_recv()
+            piece = buf.at[y_up, (me.zl + 4 - d - 2) % 4]
+            ring.rest.add(piece, piece, down)
+        return [ring.rest]
+
+    around_y(kbuf, kz, kring)
+    vz = [links.copy(trip.at[share(z, 1536)], vbuf.at[me.y, me.zl], dev) for z, dev in along_z]
+    rest = relay_y(kbuf, kring)
     w_r.over_y()
-    for q in qz:
-        q.wait_recv()
-    vz = [links.copy(trip.at[share(z, 1536)], vbuf.at[me.y, me.zl], dev) for z, dev in along_z]
+    qz.wait_recv()
     for k in rest:
         k.wait_recv()
 
@@ -273,56 +303,52 @@
     logits = jnp.concatenate(totals, axis=0) * scale
     for g in range(16):
         lsend[g] = logits[12 * g : 12 * g + 12]
-    parts = []
+    parts = Group(links, lrecv.at[0:15])
     for d in range(1, 16):
         g, dev = me.in_group(d)
-        parts.append(links.copy(lsend.at[g], lrecv.at[me.group()], dev))
+        parts.add(lsend.at[g], lrecv.at[me.group()], dev)
     lrecv[me.group()] = lsend[me.group()]
-    w_q.over_z()
-    w_c.over_z()
-    for part in parts:
-        part.wait_recv()
+    v_load.wait()
+    vring = Ring(me, links, vbuf, up, down)
+    vring.send(0)
+    around_y(vbuf, vz, vring)
+    parts.wait_recv()
     total = lrecv[0]
     for g in range(1, 16):
         total = total + lrecv[g]
     erecv[me.zh] = total
-    parts = []
+    parts = Group(links, erecv.at[0:3])
     for d in (2, 1, 3):
         slot = erecv.at[me.zh]
-        parts.append(links.copy(slot, slot, me.at(zh=(me.zh + d) % 4)))
-    v_load.wait()
-    vups, vdowns = [], []
-    around_y(vbuf, vz, vups, vdowns)
+        parts.add(slot, slot, me.at(zh=(me.zh + d) % 4))
     w_r.relay_y()
     w_r.near_x()
-    for part in parts:
-        part.wait_recv()
+    parts.wait_recv()
     total = erecv[0]
     for e in range(1, 4):
         total = total + erecv[e]
     top = jnp.max(total, axis=1, keepdims=True)
     grown = jnp.exp(total - top)
     pbuf[me.group()] = grown / jnp.sum(grown, axis=1, keepdims=True)
-    parts = []
+    parts = Group(links, pbuf.at[0:15])
     for d in range(1, 16):
         _, dev = me.in_group(d)
         slot = pbuf.at[me.group()]
-        parts.append(links.copy(slot, slot, dev))
-    vrest = relay_y(vbuf, vups, vdowns)
+        parts.add(slot, slot, dev)
+    vrest = relay_y(vbuf, vring)
+    w_q.over_z()
+    w_c.over_z()
     w_r.far_y()
     w_r.far_x()
     w_cores = [w_r.to_core(core, half)]
-    w_q.over_y()
-    for mark in marks:
-        mark.wait_recv()
-    marked = mslot[0]
-    for e in range(1, 8):
-        marked = marked + mslot[e]
-    mx[me.x] = marked
-    marks = []
-    for d in range(1, 4):
-        marks.append(links.copy(mx.at[me.x], mx.at[me.x], me.at(x=(me.x + d) % 4)))
-    for part in vrest + parts:
+    marks.wait_recv()
+    mx[me.x * 2 + me.co] = mslot[0] + mslot[1] + mslot[2] + mslot[3]
+    marks = Group(links, mx.at[0:7])
+    slot = mx.at[me.x * 2 + me.co]
+    for d in range(1, 8):
+        g = (me.x * 2 + me.co + d) % 8
+        marks.add(slot, slot, me.at(x=g // 2, co=g % 2))
+    for part in vrest + [parts]:
         part.wait_recv()
     all_probs = jnp.concatenate([pbuf[g] for g in range(16)], axis=0).astype(BF16)
 
@@ -340,15 +366,16 @@
         return carry
 
     lax.fori_loop(0, 8, context, 0)
-    back = [links.copy(csend.at[z], crecv.at[me.zl], dev) for z, dev in along_z]
+    back = Group(links, crecv.at[0:3])
+    for z, dev in along_z:
+        back.add(csend.at[z], crecv.at[me.zl], dev)
     crecv[me.zl] = csend[me.zl]
     w_r.arrive()
     w_cores.append(w_r.to_core(core, other_half))
-    w_q.relay_y()
-    w_c.over_y()
+    w_q.over_y()
     for made in last_loads:
         made.wait()
-    for made in back + w_cores:
+    for made in [back] + w_cores:
         made.wait_recv()
 
     mixed = emb_in[...].reshape(128, 768).astype(F32)
@@ -384,42 +411,41 @@
     def there(d):
         return (me.zh + d) % 4
 
-    own = [
-        links.copy(nsend.at[pair, there(d)], nb.at[me.x, me.co, me.zh], me.at(zh=there(d)))
-        for d in order
-    ]
+    own = Group(links, nb.at[0, 0, 0:3])
+    for d in order:
+        own.add(nsend.at[pair, there(d)], nb.at[me.x, me.co, me.zh], me.at(zh=there(d)))
     nb[me.x, me.co, me.zh] = nsend[pair, me.zh]
     crossed.wait_recv()
     far = [
         links.copy(xr.at[there(d)], nb.at[x_over, me.co, me.zh], me.at(zh=there(d))) for d in order
     ]
     nb[x_over, me.co, me.zh] = xr[me.zh]
-    w_q.far_y()
-    w_q_core = w_q.to_core(core, core_half)
-    w_c.relay_y()
-    for made in own:
-        made.wait_recv()
+    w_q.relay_y()
+    w_c.over_y()
+    own.wait_recv()
     piece = nb.at[me.x, me.co]
     to_mate = [links.copy(piece, piece, mate)]
-    to_core = [links.copy(piece, piece, core)]
+    to_core = Group(links, nb.at[:, 0])
+    to_core.add(piece, piece, core)
     for n, d in ((None, 0), (1, 1), (2, 3), (0, 2)):
         if n is not None:
             far[n].wait_recv()
         piece = nb.at[x_over, me.co, (me.zh + 4 - d) % 4]
         to_mate.append(links.copy(piece, piece, mate))
-        to_core.append(links.copy(piece, piece, core))
+        to_core.add(piece, piece, core)
+    w_q.far_y()
+    w_q_core = w_q.to_core(core, core_half)
+    w_c.relay_y()
     to_mate[0].wait_recv()
     piece = nb.at[x_mate, me.co]
-    to_core.append(links.copy(piece, piece, core))
+    to_core.add(piece, piece, core)
     for n, d in enumerate((0, 1, 3, 2)):
         to_mate[n + 1].wait_recv()
         piece = nb.at[3 - x_mate, me.co, (me.zh + 4 - d) % 4]
-        to_core.append(links.copy(piece, piece, core))
-    w_c.far_y()
-    w_c_core = w_c.to_core(core, slice(None))
+        to_core.add(piece, piece, core)
     w_q_core.wait_recv()
-    for made in marks + to_core:
-        made.wait_recv()
+    marks.wait_recv()
+    to_core.wait_recv()
 
     tokens = nb[...].reshape(512, 768)
     w_kv = wqbuf[:, :, :, :, 384:1152].reshape(768, 768)
@@ -433,46 +459,39 @@
     for p in range(3):
         qc[p] = queries[:, 128 * p : 128 * p + 128]
 
-    everywhere = jnp.concatenate([mx[x] for x in range(4)], axis=1)
+    everywhere = jnp.concatenate([mx[2 * x] + mx[2 * x + 1] for x in range(4)], axis=1)
     column = lax.broadcasted_iota(jnp.int32, (8, 512), 0) == 2 * me.zh + pair
     keep = jnp.sum(jnp.where(column, everywhere, 0.0), axis=0, keepdims=True) > 0
 
-    def attend(p, carry):
-        k, v = kc[p], vc[p]
-        for b in range(4):
-            q = qc[p, 64 * b : 64 * b + 64]
+    mine = 8 * (me.x % 2) + 2 * me.zh + pair
+    backs = Group(links, arecv.at[0:15])
+    for e in (2, 1, 3, 0):
+        x = (me.x + e) % 4
+        for p in range(3):
+            q = qc[p, pl.ds(pl.multiple_of(64 * x, 64), 64)]
             both = jnp.concatenate([q * low_b, q * high_b], axis=0)
             scores = lax.dot_general(
-                both, k, (((1,), (1,)), ((), ())), preferred_element_type=F32
+                both, kc[p], (((1,), (1,)), ((), ())), preferred_element_type=F32
             ) * (1.0 / math.sqrt(DH))
             scores = jnp.where(keep, scores, -1000000000.0)
             grown = jnp.exp(scores - jnp.max(scores, axis=1, keepdims=True))
             size = jnp.sum(grown, axis=1, keepdims=True)
-            made = jnp.dot(grown.astype(BF16), v, preferred_element_type=F32) / size
+            made = jnp.dot(grown.astype(BF16), vc[p], preferred_element_type=F32) / size
             made = jnp.where(low, made[:64], made[64:]).astype(BF16)
-            asend[b, p] = made.reshape(4, 16, 128)
-        return carry
-
-    lax.fori_loop(0, 3, attend, 0)
-
-    mine = 2 * me.zh + pair
-    backs = []
-    for d in (2, 1, 3, 0):
-        zh = (me.zh + d) % 4
-        for e in (2, 1, 3, 0):
+            asend[x, p] = made.reshape(4, 16, 128)
+        for d in (2, 1, 3, 0):
             if d == e == 0:
                 continue
-            x = (me.x + e) % 4
-            backs.append(
-                links.copy(asend.at[x, :, zh], arecv.at[mine, me.x % 2], me.at(x=x, zh=zh))
-            )
-    arecv[mine, me.x % 2] = asend[me.x, :, me.zh]
-    for made in backs:
-        made.wait_recv()
+            zh = (me.zh + d) % 4
+            backs.add(asend.at[x, :, zh], arecv.at[mine], me.at(x=x, zh=zh))
+    w_c.far_y()
+    w_c_core = w_c.to_core(core, slice(None))
+    arecv[mine] = asend[me.x, :, me.zh]
+    backs.wait_recv()
     w_c_core.wait_recv()
     turn_back = (above == (along % 16) * 8 + along // 16).astype(F32).astype(BF16)
     attended = jnp.concatenate(
-        [arecv[:, h, p].reshape(128, 128) for h in range(2) for p in range(3)], axis=1
+        [arecv[8 * h : 8 * h + 8, p].reshape(128, 128) for h in range(2) for p in range(3)], axis=1
     )
     attended = jnp.dot(turn_back, attended, preferred_element_type=F32).astype(BF16)
     for n in range(2):
@@ -484,7 +503,7 @@
 
 def per_device(emb, trip, occ, wr, wq, wc, gain):
     vmem = pl.BlockSpec(memory_space=pltpu.VMEM)
-    n = 160
+    n = 52
     out = pl.pallas_call(
         layer_kernel,
         out_shape=jax.ShapeDtypeStruct((128, 768), F32),
@@ -505,8 +524,8 @@
             pltpu.VMEM((2, 4, 4, 6, 8, 384), BF16),
             pltpu.VMEM((2, 4, 4, 6, 8, 384), BF16),
             pltpu.VMEM((4, 4, 6, 8, 1152), BF16),
+            pltpu.VMEM((4, 8, 128), F32),
             pltpu.VMEM((8, 8, 128), F32),
-            pltpu.VMEM((4, 8, 128), F32),
             pltpu.VMEM((128, 768), F32),
             pltpu.VMEM((2, 4, 16, 768), BF16),
             pltpu.VMEM((4, 16, 768), BF16),
@@ -515,7 +534,7 @@
             pltpu.VMEM((3, 512, 128), BF16),
             pltpu.VMEM((3, 256, 128), BF16),
             pltpu.VMEM((4, 3, 4, 16, 128), BF16),
-            pltpu.VMEM((8, 2, 3, 16, 128), BF16),
+            pltpu.VMEM((16, 3, 16, 128), BF16),
             pltpu.VMEM((8, 16), jnp.int32),
             pltpu.VMEM((16, 8, 768), BF16),
             pltpu.VMEM((768,), F32),

time: 99.8 us -> 98.2 us (0.984)
  Pallas kernels: 97.9 us -> 96.3 us
    pallas_call x1, Pallas kernels: 97.9 us -> 96.3 us  [per_device(): pl.pallas_call(layer_kernel, out_shape=jax.ShapeDtypeStruct((128, 768), F...]
where the time goes in v4:
time: 98.2 us; the launch traced here: 98.1 us
  Pallas kernels  96.3 us (98%)
  local copies, waits for them, and re-layouts  1.77 us (2%)
    pallas_call x1, Pallas kernels, per_device(): pl.pallas_call(layer_kernel, out_shape=jax.ShapeDtypeStruct((128, 768), F...  96.3 us

profile of v4, /device:TPU:1, one launch (start us, length us, event | category | flops | bytes accessed | tf_op | source)
XLA Modules:
  0.0 98.1 jit_solution(3045646218992908238)
XLA Ops:
  0.0 96.3 %msa_layer.1 = f32[128,768]{1,0:T(8,128)} custom-call(bf16[16,8,768]{2,1,0:T(8,128)(2,1)} %emb.1, bf16[16,8,2304]{2,1,0:T(8,128)(2,1)} %trip.1, s32[8,16]{1,0:T(8,128)} %bitcast.9, bf16[6,8,768]{2,1,0:T(8,128)(2,1)} %bitcast.7, bf16[6,8,2304]{2,1,0:T(8,128)(2,1)} %bitcast.6, bf16[6,8,768]{2,1,0:T(8,128)(2,1)} %bitcast.8, f32[768]{0:T(1024)} %gain.1), custom_call_target="tpu_custom_call" | custom-call | tf_op jit(solution)/shard_map/msa_layer/pallas_call | solution.py:507
  96.3 1.8 %copy.9 = f32[16,8,768]{2,1,0:T(8,128)} copy(f32[16,8,768]{2,1,0:T(8,128)} %bitcast.5) | data formatting | bytes 786432

commit v5 on v4

--- a/solution.py
+++ b/solution.py
@@ -76,6 +76,10 @@
     def group(self):
         return self.x * 4 + self.co * 2 + self.zl % 2
 
+    def on_ring(self, d):
+        z = (4 * self.zh + self.zl + d + 16) % 16
+        return self.at(zh=z // 4, zl=z % 4)
+
     def in_group(self, d):
         g = (self.group() + d) % 16
         return g, self.at(x=g // 4, co=(g // 2) % 2, zl=(self.zl // 2) * 2 + g % 2)
@@ -100,8 +104,8 @@
     def over_z(self):
         piece = self.buf.at[self.me.y, self.me.zl, self.rows]
         self.z = Group(self.links, self.buf.at[0, 0:3, self.rows])
-        for d in (1, 3, 2):
-            self.z.add(piece, piece, self.me.at(zl=(self.me.zl + d) % 4))
+        for d in (1, -1, 2):
+            self.z.add(piece, piece, self.me.on_ring(d))
 
     def over_y(self):
         self.z.wait_recv()
@@ -138,20 +142,15 @@
         return self.send(self.buf.at[:, :, rows], core)
 
 
-class Ring:
-    def __init__(self, me, links, buf, up, down):
-        self.me, self.links, self.buf, self.up, self.down = me, links, buf, up, down
-        self.ups, self.downs = {}, {}
-        self.rest = Group(links, buf.at[0:2])
+class Direct:
+    def __init__(self, me, links, buf, others):
+        self.me, self.links, self.buf, self.others = me, links, buf, others
+        self.rest = Group(links, buf.at[0:3])
 
     def send(self, d):
         piece = self.buf.at[self.me.y, (self.me.zl + 4 - d) % 4]
-        if d < 2:
-            self.ups[d] = self.links.copy(piece, piece, self.up)
-            self.rest.add(piece, piece, self.down)
-        else:
-            self.rest.add(piece, piece, self.up)
-            self.downs[d] = self.links.copy(piece, piece, self.down)
+        for device in self.others:
+            self.rest.add(piece, piece, device)
 
 
 def layer_kernel(
@@ -165,7 +164,9 @@
     along_z = [((me.zl + d) % 4, me.at(zl=(me.zl + d) % 4)) for d in range(1, 4)]
     y_up, y_down = (me.y + 1) % 4, (me.y + 3) % 4
     up, down = me.at(y=y_up), me.at(y=y_down)
-    everyone = [d for _, d in along_z] + [up, down] + [me.in_group(d)[1] for d in range(1, 16)]
+    across = me.at(y=(me.y + 2) % 4)
+    everyone = [d for _, d in along_z] + [up, down, across] + [me.in_group(d)[1] for d in range(1, 16)]
+    everyone += [me.on_ring(d) for d in (1, -1, 2, -2)]
     for d in range(1, 4):
         zh = (me.zh + d) % 4
         for e in range(4):
@@ -214,7 +215,7 @@
 
     kz = [links.copy(trip.at[share(z, 768)], kbuf.at[me.y, me.zl], dev) for z, dev in along_z]
     k_load.wait()
-    kring = Ring(me, links, kbuf, up, down)
+    kring = Direct(me, links, kbuf, (across, up, down))
     kring.send(0)
 
     for made in q_loads:
@@ -258,19 +259,9 @@
             arrivals[d - 1].wait_recv()
             ring.send(d)
 
-    def relay_y(buf, ring):
-        for d in range(2):
-            ring.ups[d].wait_recv()
-            piece = buf.at[y_down, (me.zl + 4 - d) % 4]
-            ring.rest.add(piece, piece, up)
-            ring.downs[d + 2].wait_recv()
-            piece = buf.at[y_up, (me.zl + 4 - d - 2) % 4]
-            ring.rest.add(piece, piece, down)
-        return [ring.rest]
-
     around_y(kbuf, kz, kring)
     vz = [links.copy(trip.at[share(z, 1536)], vbuf.at[me.y, me.zl], dev) for z, dev in along_z]
-    rest = relay_y(kbuf, kring)
+    rest = [kring.rest]
     w_r.over_y()
     qz.wait_recv()
     for k in rest:
@@ -309,9 +300,11 @@
         parts.add(lsend.at[g], lrecv.at[me.group()], dev)
     lrecv[me.group()] = lsend[me.group()]
     v_load.wait()
-    vring = Ring(me, links, vbuf, up, down)
+    vring = Direct(me, links, vbuf, (across, up, down))
     vring.send(0)
     around_y(vbuf, vz, vring)
+    w_q.over_z()
+    w_c.over_z()
     parts.wait_recv()
     total = lrecv[0]
     for g in range(1, 16):
@@ -335,9 +328,7 @@
         _, dev = me.in_group(d)
         slot = pbuf.at[me.group()]
         parts.add(slot, slot, dev)
-    vrest = relay_y(vbuf, vring)
-    w_q.over_z()
-    w_c.over_z()
+    vrest = [vring.rest]
     w_r.far_y()
     w_r.far_x()
     w_cores = [w_r.to_core(core, half)]

time: 98.2 us -> 94.1 us (0.958)
  Pallas kernels: 96.3 us -> 92.2 us
    pallas_call x1, Pallas kernels: 96.3 us -> 92.2 us  [per_device(): pl.pallas_call(layer_kernel, out_shape=jax.ShapeDtypeStruct((128, 768), F...]
where the time goes in v5:
time: 94.1 us; the launch traced here: 93.9 us
  Pallas kernels  92.2 us (98%)
  local copies, waits for them, and re-layouts  1.77 us (2%)
    pallas_call x1, Pallas kernels, per_device(): pl.pallas_call(layer_kernel, out_shape=jax.ShapeDtypeStruct((128, 768), F...  92.2 us

profile of v5, /device:TPU:1, one launch (start us, length us, event | category | flops | bytes accessed | tf_op | source)
XLA Modules:
  0.0 93.9 jit_solution(11815064029597642116)
XLA Ops:
  0.0 92.2 %msa_layer.1 = f32[128,768]{1,0:T(8,128)} custom-call(bf16[16,8,768]{2,1,0:T(8,128)(2,1)} %emb.1, bf16[16,8,2304]{2,1,0:T(8,128)(2,1)} %trip.1, s32[8,16]{1,0:T(8,128)} %bitcast.9, bf16[6,8,768]{2,1,0:T(8,128)(2,1)} %bitcast.7, bf16[6,8,2304]{2,1,0:T(8,128)(2,1)} %bitcast.6, bf16[6,8,768]{2,1,0:T(8,128)(2,1)} %bitcast.8, f32[768]{0:T(1024)} %gain.1), custom_call_target="tpu_custom_call" | custom-call | tf_op jit(solution)/shard_map/msa_layer/pallas_call | solution.py:498
  92.2 1.8 %copy.9 = f32[16,8,768]{2,1,0:T(8,128)} copy(f32[16,8,768]{2,1,0:T(8,128)} %bitcast.5) | data formatting | bytes 786432

commit v6 on v5

--- a/solution.py
+++ b/solution.py
@@ -396,6 +396,7 @@
     x_mate = (me.x // 2) * 2 + 1 - me.x % 2
     x_over = 3 - me.x
     mate, over = me.at(x=x_mate), me.at(x=x_over)
+    mate_core = me.at(x=x_mate, co=1 - me.co)
     crossed = links.copy(nsend.at[1 - pair], xr, over)
     order = (2, 1, 3)
 
@@ -423,6 +424,7 @@
             far[n].wait_recv()
         piece = nb.at[x_over, me.co, (me.zh + 4 - d) % 4]
         to_mate.append(links.copy(piece, piece, mate))
+        to_core.add(piece, piece, mate_core)
         to_core.add(piece, piece, core)
     w_q.far_y()
     w_q_core = w_q.to_core(core, core_half)
@@ -430,10 +432,8 @@
     to_mate[0].wait_recv()
     piece = nb.at[x_mate, me.co]
     to_core.add(piece, piece, core)
-    for n, d in enumerate((0, 1, 3, 2)):
-        to_mate[n + 1].wait_recv()
-        piece = nb.at[3 - x_mate, me.co, (me.zh + 4 - d) % 4]
-        to_core.add(piece, piece, core)
+    for made in to_mate[1:]:
+        made.wait_recv()
     w_q_core.wait_recv()
     marks.wait_recv()
     to_core.wait_recv()

time: 94.1 us -> 93.2 us (level)
  no operation moved by 1% of the time
where the time goes in v6:
time: 93.2 us; the launch traced here: 93 us
  Pallas kernels  91.3 us (98%)
  local copies, waits for them, and re-layouts  1.77 us (2%)
    pallas_call x1, Pallas kernels, per_device(): pl.pallas_call(layer_kernel, out_shape=jax.ShapeDtypeStruct((128, 768), F...  91.3 us

profile of v6, /device:TPU:1, one launch (start us, length us, event | category | flops | bytes accessed | tf_op | source)
XLA Modules:
  0.0 93.0 jit_solution(5835153578451755778)
XLA Ops:
  0.0 91.3 %msa_layer.1 = f32[128,768]{1,0:T(8,128)} custom-call(bf16[16,8,768]{2,1,0:T(8,128)(2,1)} %emb.1, bf16[16,8,2304]{2,1,0:T(8,128)(2,1)} %trip.1, s32[8,16]{1,0:T(8,128)} %bitcast.9, bf16[6,8,768]{2,1,0:T(8,128)(2,1)} %bitcast.7, bf16[6,8,2304]{2,1,0:T(8,128)(2,1)} %bitcast.6, bf16[6,8,768]{2,1,0:T(8,128)(2,1)} %bitcast.8, f32[768]{0:T(1024)} %gain.1), custom_call_target="tpu_custom_call" | custom-call | tf_op jit(solution)/shard_map/msa_layer/pallas_call | solution.py:498
  91.3 1.8 %copy.9 = f32[16,8,768]{2,1,0:T(8,128)} copy(f32[16,8,768]{2,1,0:T(8,128)} %bitcast.5) | data formatting | bytes 786432
